TPU v7x, 32 devices: a whole 2x2x4 slice. The times are simulated.
32 devices in a mesh: dp: 4 (over z), mp: 8 (over y, x, core).
Axes of the slice: x: 2, y: 2, z: 4, core: 2. Of those that a mesh axis runs over, the one named last changes fastest.
Arguments:
- guess_vectors: bfloat16 [128, 16, 4096], P(('dp', 'mp')), may hold values from -6 to 6
- preceding_symbol_vector: bfloat16 [128, 4096], P(('dp', 'mp')), may hold values from -6 to 6
- earlier_memory_matrix: float32 [128, 64, 64, 64], P('dp', 'mp'), may hold values from -4 to 4
- lag_blend_factor: float32 [4096], replicated, may hold values from 0 to 1
- constant_lag_blends: float32 [5, 4096], replicated, may hold values from 0 to 1
- blending_lower_matrix: bfloat16 [4096, 160], replicated, may hold values from -0.09375 to 0.09375
- blending_raise_matrix: bfloat16 [5, 32, 4096], replicated, may hold values from -1 to 1
- constant_fading: float32 [4096], P('mp'), may hold values from -6 to -1
- fading_lower_matrix: bfloat16 [4096, 64], replicated, may hold values from -0.09375 to 0.09375
- fading_raise_matrix: bfloat16 [64, 4096], P(None, 'mp'), may hold values from -1 to 1
- diagonal_boost: float32 [64, 64], P('mp'), may hold values from -3 to 3
- acceptor_matrix: bfloat16 [4096, 4096], P('dp', 'mp'), may hold values from -0.09375 to 0.09375
- lookup_matrix: bfloat16 [4096, 4096], P('dp', 'mp'), may hold values from -0.09375 to 0.09375
- payload_matrix: bfloat16 [4096, 4096], P('dp', 'mp'), may hold values from -0.09375 to 0.09375
- gating_matrix: bfloat16 [4096, 4096], P('dp', 'mp'), may hold values from -0.09375 to 0.09375
- emission_matrix: bfloat16 [4096, 4096], P('mp', 'dp'), may hold values from -0.09375 to 0.09375
- groupwise_scaling_factor: float32 [4096], P('mp'), may hold values from 0.1 to 1.9
- groupwise_scaling_offset: float32 [4096], P('mp'), may hold values from -3 to 3
- usable_guess_amount: int32 [128], replicated, may hold values from 1 to 16, as said below
- approved_guesses: int32 [128], replicated, may hold values from 0 to 16, as said below
- destination_slot: int32 [128], replicated, may hold values from 0 to 127, as said below
Outputs:
- layer_out: bfloat16 [128, 16, 4096], P(('dp', 'mp'))
- next_state: float32 [128, 64, 64, 64], P('dp', 'mp')
- next_edge: bfloat16 [128, 4096], P('dp', 'mp')
Inputs may be any that keep to these rules, and one draw needn't show every extreme that they name: `usable_guess_amount`: some request has all 16 draft tokens valid. approved_guesses[b] <= usable_guess_amount[b]; some request accepts all 16. destination_slot is a permutation of the requests. Of the 32 requests of one aligned block, at most 16 have owner slots in one aligned block of 32 slots, and some pair of blocks reaches 16.
All inputs are finite; a program needn't handle non-finite values.
Results may differ from a plain program's by a relative error of at most 0.007.
Values may be sent and summed in bfloat16 or wider, within the bound.
A program may use at most 256 MiB of HBM per device.

v0:
```python
import jax
import jax.numpy as jnp
from jax import lax
from jax.sharding import PartitionSpec as P

GROUP_DIMENSION = 64


norm_eps = 0.00064


def token_mixes(
    guess_vectors,
    edges,
    lag_blend_factor,
    constant_lag_blends,
    blending_lower_matrix,
    blending_raise_matrix,
):
    previous = jnp.concatenate([edges[:, None, :], guess_vectors[:, :-1, :]], axis=1)
    width = guess_vectors.shape[-1]
    current_input = guess_vectors.reshape(-1, width).astype(jnp.float32)
    shift_difference = previous.reshape(-1, width).astype(jnp.float32) - current_input
    shift_blended = (current_input + shift_difference * lag_blend_factor).astype(jnp.bfloat16)
    mixing_inner_all = jnp.tanh(
        jnp.dot(shift_blended, blending_lower_matrix, preferred_element_type=jnp.float32)
    ).astype(jnp.bfloat16)
    mixing_inner_width = blending_raise_matrix.shape[1]
    shift_mixed_rows = []
    for mix_component in range(5):
        mixing_inner_part = jnp.dot(
            mixing_inner_all[
                :, mix_component * mixing_inner_width : (mix_component + 1) * mixing_inner_width
            ],
            blending_raise_matrix[mix_component],
            preferred_element_type=jnp.float32,
        )
        shift_mixed_rows.append(
            (
                current_input
                + shift_difference * (constant_lag_blends[mix_component] + mixing_inner_part)
            ).astype(jnp.bfloat16)
        )
    return shift_mixed_rows


def wkv_blocks(
    acceptor_vectors,
    lookup_vectors,
    payload_vectors,
    logarithmic_fading_entries,
    diagonal_boost,
    starting_memory,
    approved_guesses,
):
    draft = acceptor_vectors.shape[1]
    cumulative = jnp.cumsum(logarithmic_fading_entries, axis=1)
    starts = jnp.concatenate(
        [jnp.zeros_like(logarithmic_fading_entries[:, :1]), cumulative], axis=1
    )
    before = starts[:, :draft]
    from_start = jnp.einsum(
        "bthi,bhij->bthj",
        acceptor_vectors * jnp.exp(before),
        starting_memory,
        precision=lax.Precision.HIGHEST,
    )
    later = jnp.arange(draft)[:, None] > jnp.arange(draft)[None, :]
    exponent = before[:, :, None] - cumulative[:, None, :]
    exponent = jnp.where(later[None, :, :, None, None], exponent, -1e30)
    scores = jnp.sum(
        acceptor_vectors[:, :, None] * lookup_vectors[:, None, :] * jnp.exp(exponent), axis=-1
    )
    inner = jnp.einsum("btsh,bshj->bthj", scores, payload_vectors, precision=lax.Precision.HIGHEST)
    diagonal_boost_contribution = (
        jnp.sum(acceptor_vectors * diagonal_boost * lookup_vectors, axis=-1, keepdims=True)
        * payload_vectors
    )
    outputs = from_start + inner + diagonal_boost_contribution
    at_accept = jnp.take_along_axis(starts, approved_guesses[:, None, None, None], axis=1)[:, 0]
    used = jnp.arange(draft)[None, :] < approved_guesses[:, None]
    coef_exp = jnp.where(used[:, :, None, None], at_accept[:, None] - cumulative, -1e30)
    weighted = jnp.exp(coef_exp) * lookup_vectors
    picked = jnp.exp(at_accept)[..., None] * starting_memory + jnp.einsum(
        "bshi,bshj->bhij", weighted, payload_vectors, precision=lax.Precision.HIGHEST
    )
    return (outputs, picked)


def gated_norm(outputs, gate_raw, gain, bias):
    centre = jnp.mean(outputs, axis=-1, keepdims=True)
    spread = outputs - centre
    variance = jnp.mean(spread * spread, axis=-1, keepdims=True)
    normed = (spread * lax.rsqrt(variance + norm_eps)).reshape(outputs.shape[0], -1)
    return ((normed * gain + bias) * jax.nn.silu(gate_raw)).astype(jnp.bfloat16)


def on_device(
    guess_vectors,
    preceding_symbol_vector,
    earlier_memory_matrix,
    lag_blend_factor,
    constant_lag_blends,
    blending_lower_matrix,
    blending_raise_matrix,
    constant_fading,
    fading_lower_matrix,
    fading_raise_matrix,
    diagonal_boost,
    acceptor_matrix,
    lookup_matrix,
    payload_matrix,
    gating_matrix,
    emission_matrix,
    groupwise_scaling_factor,
    groupwise_scaling_offset,
    usable_guess_amount,
    approved_guesses,
    destination_slot,
):
    own_reqs, draft, width = guess_vectors.shape
    group_count = lax.axis_size("mp")
    row_groups = lax.axis_size("dp")
    row_reqs = own_reqs * group_count
    row_index = lax.axis_index("dp")
    group_index = lax.axis_index("mp")
    local_width = acceptor_matrix.shape[1]
    local_heads = local_width // GROUP_DIMENSION
    gathered, edges_all = (
        lax.all_gather(guess_vectors, "mp", axis=0, tiled=True),
        lax.all_gather(preceding_symbol_vector, "mp", axis=0, tiled=True),
    )
    shift_mixed_rows = token_mixes(
        gathered,
        edges_all,
        lag_blend_factor,
        constant_lag_blends,
        blending_lower_matrix,
        blending_raise_matrix,
    )
    token_rows = row_reqs * draft
    sources = (shift_mixed_rows[3], shift_mixed_rows[1], shift_mixed_rows[2], shift_mixed_rows[4])
    pieces = (
        lax.all_gather(acceptor_matrix, "dp", axis=0, tiled=True),
        lax.all_gather(lookup_matrix, "dp", axis=0, tiled=True),
        lax.all_gather(payload_matrix, "dp", axis=0, tiled=True),
        lax.all_gather(gating_matrix, "dp", axis=0, tiled=True),
    )
    acceptor_vectors, lookup_vectors, payload_vectors, gate_raw = tuple(
        (
            jnp.dot(source_rows, piece, preferred_element_type=jnp.float32)
            for source_rows, piece in zip(sources, pieces)
        )
    )
    decay_inner_rows = jnp.tanh(
        jnp.dot(shift_mixed_rows[0], fading_lower_matrix, preferred_element_type=jnp.float32)
    ).astype(jnp.bfloat16)
    logarithmic_fading_entries = -jnp.exp(
        constant_fading
        + jnp.dot(decay_inner_rows, fading_raise_matrix, preferred_element_type=jnp.float32)
    )

    def to_heads(values):
        return values.reshape(row_reqs, draft, local_heads, GROUP_DIMENSION)

    row_accepted = lax.dynamic_slice_in_dim(approved_guesses, row_index * row_reqs, row_reqs)
    outputs, picked = wkv_blocks(
        to_heads(acceptor_vectors),
        to_heads(lookup_vectors),
        to_heads(payload_vectors),
        to_heads(logarithmic_fading_entries),
        diagonal_boost,
        earlier_memory_matrix,
        row_accepted,
    )
    hidden = gated_norm(
        outputs.reshape(token_rows, local_heads, GROUP_DIMENSION),
        gate_raw,
        groupwise_scaling_factor,
        groupwise_scaling_offset,
    )
    out_cols = lax.all_gather(emission_matrix, "dp", axis=1, tiled=True)
    attended = lax.psum_scatter(
        jnp.dot(hidden, out_cols, preferred_element_type=jnp.float32).astype(jnp.bfloat16),
        "mp",
        scatter_dimension=0,
        tiled=True,
    ).astype(jnp.float32)
    own_start = (row_index * group_count + group_index) * own_reqs
    own_lengths = lax.dynamic_slice_in_dim(usable_guess_amount, own_start, own_reqs)
    valid_mask = jnp.arange(draft, dtype=jnp.int32)[None, :] < own_lengths[:, None]
    layer_out = (
        guess_vectors.astype(jnp.float32)
        + jnp.where(
            valid_mask[..., None],
            attended.reshape(own_reqs, draft, width),
            jnp.zeros((), jnp.float32),
        )
    ).astype(jnp.bfloat16)
    edge_rows = jnp.concatenate([edges_all[:, None, :], gathered], axis=1)
    edge_cols = lax.dynamic_slice_in_dim(edge_rows, group_index * local_width, local_width, 2)
    chosen = jnp.take_along_axis(edge_cols, row_accepted[:, None, None], axis=1)[:, 0]
    capacity = 2 * row_reqs // row_groups
    target_rows = (destination_slot // row_reqs).reshape(row_groups, row_reqs)
    onehot = (
        target_rows[:, :, None] == jnp.arange(row_groups, dtype=jnp.int32)[None, None, :]
    ).astype(jnp.int32)
    earlier = jnp.cumsum(onehot, axis=1) - onehot
    ranks = jnp.sum(earlier * onehot, axis=-1)
    my_targets = lax.dynamic_index_in_dim(target_rows, row_index, 0, keepdims=False)
    my_ranks = lax.dynamic_index_in_dim(ranks, row_index, 0, keepdims=False)
    selected = (
        my_targets[:, None, None] == jnp.arange(row_groups, dtype=jnp.int32)[None, :, None]
    ) & (my_ranks[:, None, None] == jnp.arange(capacity, dtype=jnp.int32)[None, None, :])
    source_index = jnp.sum(
        selected.astype(jnp.int32) * jnp.arange(row_reqs, dtype=jnp.int32)[:, None, None], axis=0
    )
    filled = jnp.any(selected, axis=0)
    send_state = jnp.where(
        filled[..., None, None, None], picked[source_index], jnp.zeros((), jnp.float32)
    )
    send_edge = jnp.where(
        filled[..., None], chosen[source_index].astype(jnp.float32), jnp.zeros((), jnp.float32)
    )
    recv_state, recv_edge = (
        lax.all_to_all(
            send_state.astype(jnp.bfloat16), "dp", split_axis=0, concat_axis=0, tiled=True
        ).astype(send_state.dtype),
        lax.all_to_all(
            send_edge.astype(jnp.bfloat16), "dp", split_axis=0, concat_axis=0, tiled=True
        ).astype(send_edge.dtype),
    )
    wanted = row_index * row_reqs + jnp.arange(row_reqs, dtype=jnp.int32)
    total_reqs = destination_slot.shape[0]
    matches = (destination_slot[None, :] == wanted[:, None]).astype(jnp.int32)
    which = jnp.sum(matches * jnp.arange(total_reqs, dtype=jnp.int32)[None, :], axis=1)
    flat_index = which // row_reqs * capacity + ranks.reshape(-1)[which]
    next_state = recv_state.reshape(
        row_groups * capacity, local_heads, GROUP_DIMENSION, GROUP_DIMENSION
    )[flat_index]
    next_edge = recv_edge.reshape(row_groups * capacity, local_width)[flat_index].astype(
        jnp.bfloat16
    )
    return (layer_out, next_state, next_edge)


def solution(mesh):
    in_specs = (
        P(("dp", "mp"), None, None),
        P(("dp", "mp"), None),
        P("dp", "mp", None, None),
        P(),
        P(),
        P(),
        P(),
        P("mp"),
        P(),
        P(None, "mp"),
        P("mp", None),
        P("dp", "mp"),
        P("dp", "mp"),
        P("dp", "mp"),
        P("dp", "mp"),
        P("mp", "dp"),
        P("mp"),
        P("mp"),
        P(),
        P(),
        P(),
    )
    out_specs = (P(("dp", "mp"), None, None), P("dp", "mp", None, None), P("dp", "mp"))
    return jax.shard_map(
        on_device, mesh=mesh, in_specs=in_specs, out_specs=out_specs, check_vma=False
    )
```

profile of v0, /device:TPU:0, one launch (start us, length us, event | category | flops | bytes accessed | tf_op | source)
XLA Modules:
  0.0 585.9 jit_solution(18396825524794450216)
XLA Ops:
  12.2 10.8 %all-gather = bf16[8,4,4096]{2,1,0:T(4,128)(2,1)S(1)} all-gather(bf16[1,4,4096]{2,1,0:T(4,128)(2,1)S(1)} %bitcast.122), channel_id=1, replica_groups=mesh['dp'=4,'mp'=8] {'mp'}, dimensions={0}, use_global_device_ids=true | all-gather | bytes 294912 | tf_op jit(solution)/shard_map/all_gather | solution.py:131
  23.9 25.6 %all-gather.8.cloned.1.call-done = bf16[32,16,4096]{2,1,0:T(8,128)(2,1)} async-done(((bf16[4,16,4096]{2,1,0:T(8,128)(2,1)}), bf16[32,16,4096]{2,1,0:T(8,128)(2,1)}) %all-gather.8.cloned.1.call-update) | async-done | bytes 4194320 | tf_op jit(solution)/shard_map/all_gather | solution.py:130
  49.4 3.7 pad_maximum_fusion
  53.1 1.9 copy-done.7
  55.1 2.0 fusion.28
  57.1 74.7 %all-gather.12.cloned.1.call-done = bf16[4096,512]{1,0:T(8,128)(2,1)} async-done(((bf16[1024,512]{1,0:T(8,128)(2,1)}), bf16[4096,512]{1,0:T(8,128)(2,1)}) %all-gather.12.cloned.1.call-update) | async-done | bytes 4194320 | tf_op jit(solution)/shard_map/all_gather | solution.py:146
  131.8 8.5 %fusion.23 = f32[512,512]{1,0:T(8,128)S(1)} fusion(bf16[4096,512]{1,0:T(8,128)(2,1)} %all-gather.12.cloned.1.call-done, bf16[512,4096]{1,0:T(8,128)(2,1)} %bitcast.105, bf16[512,4096]{1,0:T(8,128)(2,1)} %bitcast.112, f32[4096]{0:T(1024)S(1)} %bitcast.127, bf16[5,32,4096]{2,1,0:T(8,128)(2,1)} %param.27, bf16[512,160]{0,1:T(8,128)(2,1)S(1)} %fusion.28), kind=kOutput, calls=%fused_computation.48 | convolution fusion | flops 2296381440 | bytes 13942784 | tf_op jit(solution)/shard_map/dot_general | solution.py:151
  140.3 1.8 reshape.356
  142.2 70.5 %all-gather.14.cloned.1.call-done = bf16[4096,512]{1,0:T(8,128)(2,1)} async-done(((bf16[1024,512]{1,0:T(8,128)(2,1)}), bf16[4096,512]{1,0:T(8,128)(2,1)}) %all-gather.14.cloned.1.call-update) | async-done | bytes 4194320 | tf_op jit(solution)/shard_map/all_gather | solution.py:145
  212.7 8.6 %fusion.22 = f32[512,512]{1,0:T(8,128)S(1)} fusion(bf16[4096,512]{1,0:T(8,128)(2,1)} %all-gather.14.cloned.1.call-done, bf16[512,4096]{1,0:T(8,128)(2,1)} %bitcast.106, bf16[512,4096]{1,0:T(8,128)(2,1)} %bitcast.113, f32[4096]{0:T(1024)S(1)} %bitcast.126, bf16[5,32,4096]{2,1,0:T(8,128)(2,1)} %param.27, bf16[512,160]{0,1:T(8,128)(2,1)S(1)} %fusion.28), kind=kOutput, calls=%fused_computation.47 | convolution fusion | flops 2296381440 | bytes 13942784 | tf_op jit(solution)/shard_map/dot_general | solution.py:151
  221.3 1.8 mul.159
  223.1 6.9 %fusion.32 = bf16[512,64]{0,1:T(8,128)(2,1)S(1)} fusion(bf16[4096,64]{0,1:T(8,128)(2,1)S(1)} %copy-done.19, bf16[512,4096]{1,0:T(8,128)(2,1)} %bitcast.107, bf16[512,4096]{1,0:T(8,128)(2,1)} %bitcast.114, f32[4096]{0:T(1024)S(1)} %bitcast.125, bf16[5,32,4096]{2,1,0:T(8,128)(2,1)} %param.27, bf16[512,160]{0,1:T(8,128)(2,1)S(1)} %fusion.28), kind=kOutput, calls=%fused_computation.53 | convolution fusion | flops 417366016 | bytes 9289728 | tf_op jit(solution)/shard_map/dot_general | solution.py:156
  230.4 1.9 reshape.355
  232.3 1.8 fusion.77
  234.1 59.4 %all-gather.10.cloned.1.call-done = bf16[4096,512]{1,0:T(8,128)(2,1)} async-done(((bf16[1024,512]{1,0:T(8,128)(2,1)}), bf16[4096,512]{1,0:T(8,128)(2,1)}) %all-gather.10.cloned.1.call-update) | async-done | bytes 4194320 | tf_op jit(solution)/shard_map/all_gather | solution.py:144
  293.4 8.6 %fusion.24 = f32[512,512]{1,0:T(8,128)S(1)} fusion(bf16[4096,512]{1,0:T(8,128)(2,1)} %all-gather.10.cloned.1.call-done, bf16[512,4096]{1,0:T(8,128)(2,1)} %bitcast.108, bf16[512,4096]{1,0:T(8,128)(2,1)} %bitcast.115, f32[4096]{0:T(1024)S(1)} %bitcast.124, bf16[5,32,4096]{2,1,0:T(8,128)(2,1)} %param.27, bf16[512,160]{0,1:T(8,128)(2,1)} %copy-done.25), kind=kOutput, calls=%fused_computation.49 | convolution fusion | flops 2296381440 | bytes 13942784 | tf_op jit(solution)/shard_map/dot_general | solution.py:151
  302.0 1.7 reshape.354
  303.8 1.5 concatenate.10
  305.3 2.2 gather_fusion.5
  307.7 6.3 %exponential_multiply_fusion = (f32[32,16,8,64]{3,2,1,0:T(8,128)}, f32[32,16,8,64]{3,2,1,0:T(8,128)}, f32[32,16,8]{2,1,0:T(8,128)S(1)}, f32[32,16,8,64]{3,2,1,0:T(8,128)}) fusion(f32[32,16,8,64]{3,2,1,0:T(8,128)} %mul.159, f32[32,16,8,64]{3,2,1,0:T(8,128)S(1)} %fusion.77, f32[32,8,64]{2,1,0:T(8,128)S(1)} %get-tuple-element.4, ...), kind=kLoop, calls=%fused_computation.35 | loop fusion | flops 1830912 | bytes 6375936 | tf_op jit(solution)/shard_map/mul | solution.py:83
  314.0 15.2 %multiply_reduce_fusion = f32[32,16,16,8]{3,2,1,0:T(8,128)} fusion(f32[32,16,8,64]{3,2,1,0:T(8,128)S(1)} %fusion.77, f32[32,16,8,64]{3,2,1,0:T(8,128)} %get-tuple-element.10, f32[32,16,8,64]{3,2,1,0:T(8,128)} %mul.159, f32[32,16,8,64]{3,2,1,0:T(8,128)} %reshape.354, pred[16,16]{1,0:T(8,128)(4,1)S(1)} %iota_compare_fusion.3), kind=kLoop, calls=%fused_computation.7 | loop fusion | flops 20905984 | bytes 4456704 | tf_op jit(solution)/shard_map/reduce_sum | solution.py:71
  329.3 4.0 copy.69
  333.3 10.2 %fusion.11 = f32[32,8,16,64]{3,2,1,0:T(8,128)S(1)} fusion(f32[32,8,64,64]{3,2,1,0:T(8,128)} %param.23, f32[32,16,8,64]{3,2,1,0:T(8,128)S(1)} %copy-done.6), kind=kOutput, calls=%fused_computation.33 | convolution fusion | flops 201326592 | bytes 6291456 | tf_op jit(solution)/shard_map/bthi,bhij->bthj/dot_general | solution.py:62
  343.5 3.6 fusion.76
  347.4 1.3 multiply_reduce_fusion.1
  348.9 4.5 copy.82
  353.5 0.7 gather_fusion.6
  354.2 19.7 %multiply_add_fusion = bf16[32,8,64,64]{3,2,1,0:T(8,128)(2,1)} fusion(f32[32,8,64,64]{3,2,1,0:T(8,128)} %param.23, f32[32,8,64]{2,1,0:T(8,128)S(1)} %get-tuple-element.3, f32[32,16,8,64]{3,2,1,0:T(8,128)} %get-tuple-element.7, f32[32,16,8,64]{3,2,1,0:T(8,128)} %reshape.356), kind=kOutput, calls=%fused_computation.23 | convolution fusion | flops 204472320 | bytes 8454144 | tf_op jit(solution)/shard_map/bshi,bshj->bhij/dot_general | solution.py:84
  373.9 7.8 %gather_fusion = bf16[64,8,64,64]{3,2,1,0:T(8,128)(2,1)} fusion(bf16[32,8,64,64]{3,2,1,0:T(8,128)(2,1)} %multiply_add_fusion, s32[1024]{0:T(1024)S(1)} %pad_clamp_fusion.2), kind=kCustom, calls=%fused_computation | custom fusion | bytes 8388864 | tf_op jit(solution)/shard_map/gather | solution.py:220
  381.8 0.7 gather_fusion.3
  382.5 0.7 fusion.56
  383.2 3.5 all-to-all-start.1
  386.7 10.5 %select_convert_fusion = bf16[4,16,8,64,64]{4,3,2,1,0:T(8,128)(2,1)} fusion(bf16[4,16,8,64,64]{4,3,2,1,0:T(8,128)(2,1)} %bitcast.103, pred[4,16]{1,0:T(4,128)(4,1)S(1)} %and_reduce_fusion), kind=kLoop, calls=%fused_computation.15 | loop fusion | flops 2097152 | bytes 8388672 | tf_op jit(solution)/shard_map/convert_element_type | solution.py:227
  397.3 2.2 copy.72
  399.9 1.4 copy.79
  401.3 1.5 reshape.357
  403.4 9.7 %reshape.439 = bf16[4,2,262144]{2,1,0:T(2,128)(2,1)} reshape(bf16[4,16,8,64,64]{4,3,2,1,0:T(8,128)(2,1)} %select_convert_fusion) | data formatting | bytes 8388608
  413.1 5.1 all-to-all-start
  418.5 9.7 %multiply_convert_fusion = bf16[512,512]{1,0:T(8,128)(2,1)} fusion(bf16[4096,512]{1,0:T(8,128)(2,1)} %all-gather.16.cloned.1.call-done, bf16[512,4096]{1,0:T(8,128)(2,1)} %bitcast.109, bf16[512,4096]{1,0:T(8,128)(2,1)} %bitcast.116, f32[4096]{0:T(1024)S(1)} %bitcast.123, f32[512,512]{1,0:T(8,128)S(1)} %copy-done.12, f32[512,512]{1,0:T(8,128)S(1)} %copy-done.11, ...), kind=kOutput, calls=%fused_computation.57 | convolution fusion | flops 2299002880 | bytes 16568320 | tf_op jit(solution)/shard_map/dot_general | solution.py:151
  428.2 67.7 %all-gather.18.cloned.1.call-done = bf16[512,4096]{1,0:T(8,128)(2,1)} async-done(((bf16[512,1024]{1,0:T(8,128)(2,1)}), bf16[512,4096]{1,0:T(8,128)(2,1)}) %all-gather.18.cloned.1.call-update) | async-done | bytes 4194320 | tf_op jit(solution)/shard_map/all_gather | solution.py:182
  495.9 6.7 %convolution_convert_fusion = bf16[512,4096]{1,0:T(8,128)(2,1)} fusion(bf16[512,512]{1,0:T(8,128)(2,1)} %multiply_convert_fusion, bf16[512,4096]{1,0:T(8,128)(2,1)} %all-gather.18.cloned.1.call-done), kind=kOutput, calls=%fused_computation.24 | convolution fusion | flops 2149580800 | bytes 8912896 | tf_op jit(solution)/shard_map/dot_general | solution.py:184
  503.5 0.7 gather_fusion.1
  504.3 1.2 gather_fusion.4
  505.6 40.1 %all-to-all-done = bf16[4,2,262144]{2,1,0:T(2,128)(2,1)} async-done(((bf16[4,2,262144]{2,1,0:T(2,128)(2,1)}), bf16[4,2,262144]{2,1,0:T(2,128)(2,1)}, u32[]{:S(2)}, u32[]{:S(2)}) %all-to-all-start) | async-done | bytes 4194336 | tf_op jit(solution)/shard_map/all_to_all | solution.py:226
  545.7 9.3 %reshape.440 = bf16[4,16,8,64,64]{4,3,2,1,0:T(8,128)(2,1)} reshape(bf16[4,2,262144]{2,1,0:T(2,128)(2,1)} %all-to-all-done) | data formatting | bytes 8388608
  555.0 11.3 %bitcast_convert_fusion = f32[64,8,64,64]{3,2,1,0:T(8,128)} fusion(bf16[4,16,8,64,64]{4,3,2,1,0:T(8,128)(2,1)} %reshape.440), kind=kLoop, calls=%fused_computation.22 | loop fusion | flops 2097152 | bytes 12582912 | tf_op jit(solution)/shard_map/reshape | solution.py:238
  566.3 10.4 %gather_fusion.2 = f32[32,8,64,64]{3,2,1,0:T(8,128)} fusion(f32[64,8,64,64]{3,2,1,0:T(8,128)} %bitcast_convert_fusion, s32[1024]{0:T(1024)S(1)} %pad_clamp_fusion), kind=kCustom, calls=%fused_computation.2 | custom fusion | bytes 8388736 | tf_op jit(solution)/shard_map/gather | solution.py:238
  576.7 2.1 fusion.34
  (117 shorter events, 9.0 us)
Async XLA Ops:
  7.2 47.9 %copy-start = (bf16[4096,160]{0,1:T(8,128)(2,1)S(1)}, bf16[4096,160]{0,1:T(8,128)(2,1)}, u32[]{:S(2)}) copy-start(bf16[4096,160]{0,1:T(8,128)(2,1)} %param.26) | copy-start | bytes 3932164
  7.2 4.0 copy-start.18
  7.2 4.2 copy-start.24
  7.2 5.0 copy-start.15
  7.2 16.4 %copy-start.14 = (f32[5,4096]{1,0:T(8,128)S(1)}, f32[5,4096]{1,0:T(8,128)}, u32[]{:S(2)}) copy-start(f32[5,4096]{1,0:T(8,128)} %param.25) | copy-start | bytes 245764
  7.2 42.2 %all-gather.8.cloned.1.call-start = ((), (), s32[]{:S(2)}) async-start(), calls=%async_computation.3 | async-start | bytes 4718592 | tf_op jit(solution)/shard_map/all_gather | solution.py:130
  8.0 123.8 %all-gather.12.cloned.1.call-start = ((), (), s32[]{:S(2)}) async-start(), calls=%async_computation.5 | async-start | bytes 5242880 | tf_op jit(solution)/shard_map/all_gather | solution.py:146
  8.7 204.0 %all-gather.14.cloned.1.call-start = ((), (), s32[]{:S(2)}) async-start(), calls=%async_computation.6 | async-start | bytes 5242880 | tf_op jit(solution)/shard_map/all_gather | solution.py:145
  9.4 284.0 %all-gather.10.cloned.1.call-start = ((), (), s32[]{:S(2)}) async-start(), calls=%async_computation.4 | async-start | bytes 5242880 | tf_op jit(solution)/shard_map/all_gather | solution.py:144
  10.0 408.5 %all-gather.16.cloned.1.call-start = ((), (), s32[]{:S(2)}) async-start(), calls=%async_computation.7 | async-start | bytes 5242880 | tf_op jit(solution)/shard_map/all_gather | solution.py:147
  10.6 485.3 %all-gather.18.cloned.1.call-start = ((), (), s32[]{:S(2)}) async-start(), calls=%async_computation.8 | async-start | bytes 5242880 | tf_op jit(solution)/shard_map/all_gather | solution.py:182
  23.1 30.1 %copy-start.8 = (bf16[32,1,4096]{2,0,1:T(8,128)(2,1)}, bf16[32,1,4096]{2,0,1:T(8,128)(2,1)S(1)}, u32[]{:S(2)}) copy-start(bf16[32,1,4096]{2,0,1:T(8,128)(2,1)S(1)} %broadcast_in_dim.75) | copy-start | bytes 786436
  49.4 5.7 copy-start.3
  49.4 5.7 copy-start.20
  53.1 1.9 copy-start.7
  57.1 166.0 %copy-start.25 = (bf16[512,160]{0,1:T(8,128)(2,1)}, bf16[512,160]{0,1:T(8,128)(2,1)S(1)}, u32[]{:S(2)}) copy-start(bf16[512,160]{0,1:T(8,128)(2,1)S(1)} %fusion.28) | copy-start | bytes 491524
  212.7 10.4 %copy-start.19 = (bf16[4096,64]{0,1:T(8,128)(2,1)S(1)}, bf16[4096,64]{0,1:T(8,128)(2,1)}, u32[]{:S(2)}) copy-start(bf16[4096,64]{0,1:T(8,128)(2,1)} %param.29) | copy-start | bytes 1572868
  223.1 6.9 %copy-start.13 = (bf16[64,512]{1,0:T(8,128)(2,1)S(1)}, bf16[64,512]{1,0:T(8,128)(2,1)}, u32[]{:S(2)}) copy-start(bf16[64,512]{1,0:T(8,128)(2,1)} %param.30) | copy-start | bytes 196612
  223.1 6.9 %copy-start.17 = (f32[512]{0:T(512)S(1)}, f32[512]{0:T(512)}, u32[]{:S(2)}) copy-start(f32[512]{0:T(512)} %param.28) | copy-start | bytes 6148
  302.0 5.6 copy-start.16
  329.3 4.0 copy-start.6
  333.3 10.2 %copy-start.2 = (f32[32,16,8,64]{3,2,1,0:T(8,128)S(1)}, f32[32,16,8,64]{3,2,1,0:T(8,128)}, u32[]{:S(2)}) copy-start(f32[32,16,8,64]{3,2,1,0:T(8,128)} %reshape.356) | copy-start | bytes 3145732
  333.3 10.2 %copy-start.5 = (f32[32,16,16,8]{2,1,3,0:T(8,128)S(1)}, f32[32,16,16,8]{2,1,3,0:T(8,128)}, u32[]{:S(2)}) copy-start(f32[32,16,16,8]{2,1,3,0:T(8,128)} %copy.69) | copy-start | bytes 786436
  348.8 4.5 copy-start.9
  383.2 29.9 %all-to-all-start.1 = ((bf16[4,16,512]{2,1,0:T(8,128)(2,1)}), bf16[4,16,512]{2,1,0:T(8,128)(2,1)S(1)}, u32[]{:S(2)}, u32[]{:S(2)}) async-start(bf16[4,16,512]{2,1,0:T(8,128)(2,1)} %fusion.56), calls=%async_computation.2 | async-start | bytes 131072 | tf_op jit(solution)/shard_map/all_to_all | solution.py:229
  399.5 1.9 copy-start.4
  413.1 5.4 copy-start.11
  413.1 5.4 copy-start.12
  413.1 5.5 copy-start.21
  413.1 5.5 copy-start.22
  413.1 132.6 %all-to-all-start = ((bf16[4,2,262144]{2,1,0:T(2,128)(2,1)}), bf16[4,2,262144]{2,1,0:T(2,128)(2,1)}, u32[]{:S(2)}, u32[]{:S(2)}) async-start(bf16[4,2,262144]{2,1,0:T(2,128)(2,1)} %reshape.439), calls=%async_computation.1 | async-start | bytes 8388608 | tf_op jit(solution)/shard_map/all_to_all | solution.py:226
  418.2 158.5 %reduce-scatter.2.cloned.1.call-start = ((), (), s32[]{:S(2)}) async-start(), calls=%async_computation.9 | async-start | bytes 4718592 | tf_op jit(solution)/shard_map/reduce_scatter | solution.py:183
  502.6 0.7 copy-start.23
  566.3 10.4 %copy-start.10 = (bf16[4,16,4096]{2,1,0:T(8,128)(2,1)S(1)}, bf16[4,16,4096]{2,1,0:T(8,128)(2,1)}, u32[]{:S(2)}) copy-start(bf16[4,16,4096]{2,1,0:T(8,128)(2,1)} %param.21) | copy-start | bytes 1572868
  566.3 12.5 %copy-start.1 = (bf16[4096,160]{0,1:T(8,128)(2,1)S(1)}, bf16[4096,160]{0,1:T(8,128)(2,1)}, u32[]{:S(2)}) copy-start(bf16[4096,160]{0,1:T(8,128)(2,1)} %param.26) | copy-start | bytes 3932164
Sparse Core Ops, SparseCore 0:
  9.9 39.4 all-gather.7
  51.0 80.7 all-gather.11
  133.4 79.2 all-gather.13
  214.1 79.2 all-gather.9
  294.9 79.2 all-gather.15
  375.6 120.2 all-gather.17
  502.8 49.4 reduce-scatter.1
where the time goes:
time: 590 us; the launch traced here: 586 us
  waiting for transfers between devices  342 us (58%)
  matrix products  84.8 us (14%)
  local copies, waits for them, and re-layouts  70.2 us (12%)
  other arithmetic  54.3 us (9%)
  between operations  15 us (3%)
  blocking collectives  10.8 us (2%)
  starting transfers between devices  9.1 us (2%)
    all_gather x1, waiting for transfers between devices, on_device(): lax.all_gather(payload_matrix, 'dp', axis=0, tiled=True)  74.7 us
    all_gather x1, waiting for transfers between devices, on_device(): lax.all_gather(lookup_matrix, 'dp', axis=0, tiled=True)  70.5 us
    all_gather x1, waiting for transfers between devices, on_device(): out_cols = lax.all_gather(emission_matrix, 'dp', axis=1, tiled=True)  67.7 us
    all_gather x1, waiting for transfers between devices, on_device(): lax.all_gather(acceptor_matrix, 'dp', axis=0, tiled=True)  59.4 us
    all_to_all x1, waiting for transfers between devices, on_device(): lax.all_to_all(send_state.astype(jnp.bfloat16), 'dp', split_axis=0, conca...  40.1 us
    dot_general x4, matrix products, on_device(): jnp.dot(source_rows, piece, preferred_element_type=jnp.float32)  35.4 us
    all_gather x1, waiting for transfers between devices, on_device(): lax.all_gather(guess_vectors, 'mp', axis=0, tiled=True)  25.6 us
    unnamed x55, local copies, waits for them, and re-layouts  21.5 us
  transfers between devices with their start and end apart: 9, of which 6 were waited for; matrix products, arithmetic and copies ran while one was open for 35% of the time, Pallas kernels for 0%

commit v1 on v0

--- a/solution.py
+++ b/solution.py
@@ -9,39 +9,20 @@
 norm_eps = 0.00064
 
 
-def token_mixes(
-    guess_vectors,
-    edges,
-    lag_blend_factor,
-    constant_lag_blends,
-    blending_lower_matrix,
-    blending_raise_matrix,
-):
-    previous = jnp.concatenate([edges[:, None, :], guess_vectors[:, :-1, :]], axis=1)
-    width = guess_vectors.shape[-1]
-    current_input = guess_vectors.reshape(-1, width).astype(jnp.float32)
-    shift_difference = previous.reshape(-1, width).astype(jnp.float32) - current_input
-    shift_blended = (current_input + shift_difference * lag_blend_factor).astype(jnp.bfloat16)
-    mixing_inner_all = jnp.tanh(
-        jnp.dot(shift_blended, blending_lower_matrix, preferred_element_type=jnp.float32)
-    ).astype(jnp.bfloat16)
-    mixing_inner_width = blending_raise_matrix.shape[1]
-    shift_mixed_rows = []
-    for mix_component in range(5):
-        mixing_inner_part = jnp.dot(
-            mixing_inner_all[
-                :, mix_component * mixing_inner_width : (mix_component + 1) * mixing_inner_width
-            ],
-            blending_raise_matrix[mix_component],
-            preferred_element_type=jnp.float32,
-        )
-        shift_mixed_rows.append(
-            (
-                current_input
-                + shift_difference * (constant_lag_blends[mix_component] + mixing_inner_part)
-            ).astype(jnp.bfloat16)
-        )
-    return shift_mixed_rows
+def shift(guess_vectors, edges):
+    previous = jnp.concatenate([edges[..., None, :], guess_vectors[..., :-1, :]], axis=-2)
+    current_input = guess_vectors.astype(jnp.float32)
+    return current_input, previous.astype(jnp.float32) - current_input
+
+
+def dot32(left, right):
+    return jnp.dot(left, right, preferred_element_type=jnp.float32)
+
+
+def mix(current_input, shift_difference, constant, inner, raise_matrix):
+    return (current_input + shift_difference * (constant + dot32(inner, raise_matrix))).astype(
+        jnp.bfloat16
+    )
 
 
 def wkv_blocks(
@@ -126,38 +107,90 @@
     group_index = lax.axis_index("mp")
     local_width = acceptor_matrix.shape[1]
     local_heads = local_width // GROUP_DIMENSION
-    gathered, edges_all = (
-        lax.all_gather(guess_vectors, "mp", axis=0, tiled=True),
-        lax.all_gather(preceding_symbol_vector, "mp", axis=0, tiled=True),
-    )
-    shift_mixed_rows = token_mixes(
-        gathered,
-        edges_all,
-        lag_blend_factor,
-        constant_lag_blends,
-        blending_lower_matrix,
-        blending_raise_matrix,
-    )
+    inner_width = blending_raise_matrix.shape[1]
+    decay_width = fading_lower_matrix.shape[1]
+    own_tokens = own_reqs * draft
+    col_width = width // row_groups
+    own_current, own_difference = shift(guess_vectors, preceding_symbol_vector)
+    own_current = own_current.reshape(own_tokens, width)
+    own_difference = own_difference.reshape(own_tokens, width)
+    blended = (own_current + own_difference * lag_blend_factor).astype(jnp.bfloat16)
+    own_inner = jnp.tanh(dot32(blended, blending_lower_matrix)).astype(jnp.bfloat16)
+    own_decay_mix = mix(
+        own_current,
+        own_difference,
+        constant_lag_blends[0],
+        own_inner[:, :inner_width],
+        blending_raise_matrix[0],
+    )
+    own_decay_inner = jnp.tanh(dot32(own_decay_mix, fading_lower_matrix)).astype(jnp.bfloat16)
+    own_narrow = jnp.concatenate([own_inner, own_decay_inner], axis=1)
+    narrow_width = own_narrow.shape[1]
+    narrow_rows = own_tokens * narrow_width // col_width
+
+    def by_columns(rows):
+        return rows.reshape(-1, row_groups, col_width).transpose(1, 0, 2)
+
+    packed = jnp.concatenate(
+        [
+            by_columns(guess_vectors.reshape(own_tokens, width)),
+            by_columns(preceding_symbol_vector),
+            jnp.broadcast_to(
+                own_narrow.reshape(1, narrow_rows, col_width),
+                (row_groups, narrow_rows, col_width),
+            ),
+        ],
+        axis=1,
+    )
+    packed = lax.all_to_all(packed, "dp", split_axis=0, concat_axis=0, tiled=True)
+    packed = lax.all_gather(packed, "mp", axis=0, tiled=False)
+    packed = packed.transpose(1, 0, 2, 3)
+    tokens = packed[:, :, :own_tokens].reshape(
+        row_groups, group_count, own_reqs, draft, col_width
+    )
+    edges = packed[:, :, own_tokens : own_tokens + own_reqs]
+    narrow = packed[:, :, own_tokens + own_reqs :].reshape(
+        row_groups, group_count * own_tokens, narrow_width
+    )
+    all_tokens = row_groups * group_count * own_tokens
+    current, difference = shift(tokens, edges)
+    current = current.reshape(all_tokens, col_width)
+    difference = difference.reshape(all_tokens, col_width)
+    inner_all = narrow.reshape(all_tokens, narrow_width)
+    col_start = row_index * col_width
+    constants = lax.dynamic_slice_in_dim(constant_lag_blends, col_start, col_width, 1)
+    raises = lax.dynamic_slice_in_dim(blending_raise_matrix, col_start, col_width, 2)
+
+    def partial(component, matrix):
+        mixed = mix(
+            current,
+            difference,
+            constants[component],
+            inner_all[:, component * inner_width : (component + 1) * inner_width],
+            raises[component],
+        )
+        return dot32(mixed, matrix).astype(jnp.bfloat16)
+
+    def summed(values):
+        return lax.psum_scatter(values, "dp", scatter_dimension=0, tiled=True).astype(jnp.float32)
+
     token_rows = row_reqs * draft
-    sources = (shift_mixed_rows[3], shift_mixed_rows[1], shift_mixed_rows[2], shift_mixed_rows[4])
-    pieces = (
-        lax.all_gather(acceptor_matrix, "dp", axis=0, tiled=True),
-        lax.all_gather(lookup_matrix, "dp", axis=0, tiled=True),
-        lax.all_gather(payload_matrix, "dp", axis=0, tiled=True),
-        lax.all_gather(gating_matrix, "dp", axis=0, tiled=True),
-    )
-    acceptor_vectors, lookup_vectors, payload_vectors, gate_raw = tuple(
-        (
-            jnp.dot(source_rows, piece, preferred_element_type=jnp.float32)
-            for source_rows, piece in zip(sources, pieces)
+    triple = summed(
+        jnp.concatenate(
+            [
+                partial(3, acceptor_matrix),
+                partial(1, lookup_matrix),
+                partial(2, payload_matrix),
+            ],
+            axis=1,
         )
     )
-    decay_inner_rows = jnp.tanh(
-        jnp.dot(shift_mixed_rows[0], fading_lower_matrix, preferred_element_type=jnp.float32)
-    ).astype(jnp.bfloat16)
+    acceptor_vectors, lookup_vectors, payload_vectors = jnp.split(triple, 3, axis=1)
+    gate_raw = summed(partial(4, gating_matrix))
+    row_narrow = lax.dynamic_index_in_dim(narrow, row_index, 0, keepdims=False)
+    decay_inner_rows = row_narrow[:, narrow_width - decay_width :]
     logarithmic_fading_entries = -jnp.exp(
-        constant_fading
-        + jnp.dot(decay_inner_rows, fading_raise_matrix, preferred_element_type=jnp.float32)
+        constant_fading + dot32(decay_inner_rows, fading_raise_matrix)
     )
 
     def to_heads(values):
@@ -197,9 +230,11 @@
             jnp.zeros((), jnp.float32),
         )
     ).astype(jnp.bfloat16)
-    edge_rows = jnp.concatenate([edges_all[:, None, :], gathered], axis=1)
-    edge_cols = lax.dynamic_slice_in_dim(edge_rows, group_index * local_width, local_width, 2)
-    chosen = jnp.take_along_axis(edge_cols, row_accepted[:, None, None], axis=1)[:, 0]
+    own_accepted = lax.dynamic_slice_in_dim(approved_guesses, own_start, own_reqs)
+    edge_rows = jnp.concatenate([preceding_symbol_vector[:, None, :], guess_vectors], axis=1)
+    own_chosen = jnp.take_along_axis(edge_rows, own_accepted[:, None, None], axis=1)[:, 0]
+    chosen = lax.all_gather(own_chosen, ("dp", "mp"), axis=0, tiled=True)
+    chosen_cols = lax.dynamic_slice_in_dim(chosen, group_index * local_width, local_width, 1)
     capacity = 2 * row_reqs // row_groups
     target_rows = (destination_slot // row_reqs).reshape(row_groups, row_reqs)
     onehot = (
@@ -215,21 +250,8 @@
     source_index = jnp.sum(
         selected.astype(jnp.int32) * jnp.arange(row_reqs, dtype=jnp.int32)[:, None, None], axis=0
     )
-    filled = jnp.any(selected, axis=0)
-    send_state = jnp.where(
-        filled[..., None, None, None], picked[source_index], jnp.zeros((), jnp.float32)
-    )
-    send_edge = jnp.where(
-        filled[..., None], chosen[source_index].astype(jnp.float32), jnp.zeros((), jnp.float32)
-    )
-    recv_state, recv_edge = (
-        lax.all_to_all(
-            send_state.astype(jnp.bfloat16), "dp", split_axis=0, concat_axis=0, tiled=True
-        ).astype(send_state.dtype),
-        lax.all_to_all(
-            send_edge.astype(jnp.bfloat16), "dp", split_axis=0, concat_axis=0, tiled=True
-        ).astype(send_edge.dtype),
-    )
+    send_state = picked.astype(jnp.bfloat16)[source_index]
+    recv_state = lax.all_to_all(send_state, "dp", split_axis=0, concat_axis=0, tiled=True)
     wanted = row_index * row_reqs + jnp.arange(row_reqs, dtype=jnp.int32)
     total_reqs = destination_slot.shape[0]
     matches = (destination_slot[None, :] == wanted[:, None]).astype(jnp.int32)
@@ -237,10 +259,8 @@
     flat_index = which // row_reqs * capacity + ranks.reshape(-1)[which]
     next_state = recv_state.reshape(
         row_groups * capacity, local_heads, GROUP_DIMENSION, GROUP_DIMENSION
-    )[flat_index]
-    next_edge = recv_edge.reshape(row_groups * capacity, local_width)[flat_index].astype(
-        jnp.bfloat16
-    )
+    )[flat_index].astype(jnp.float32)
+    next_edge = chosen_cols[which]
     return (layer_out, next_state, next_edge)
 
 

time: 590 us -> 553 us (0.937)
  waiting for transfers between devices: 342 us -> 279 us
  local copies, waits for them, and re-layouts: 70.2 us -> 101 us
  blocking collectives: 10.8 us -> 24.9 us
  matrix products: 84.8 us -> 71.4 us
    reduce_scatter x0 -> x2, waiting for transfers between devices: none -> 132 us  [summed(): lax.psum_scatter(values, 'dp', scatter_dimension=0, tiled=True)]
    all_gather x5 -> x2, waiting for transfers between devices: 230 us -> 119 us  [the longest x1 76.3 us: on_device(): chosen = lax.all_gather(own_chosen, ('dp', 'mp'), axis=0, tiled=True)]
    all_gather x1, waiting for transfers between devices: 67.7 us -> 0.02 us  [on_device(): out_cols = lax.all_gather(emission_matrix, 'dp', axis=1, tiled=True)]
    all_to_all x2 -> x1, waiting for transfers between devices: 40.1 us -> 0.01 us  [on_device(): lax.all_to_all(send_state, 'dp', split_axis=0, concat_axis=0, tiled=True)]
    reduce_scatter x1, waiting for transfers between devices: 0.01 us -> 27.9 us  [on_device(): lax.psum_scatter(jnp.dot(hidden, out_cols, preferred_element_type=jnp.flo...]
    all_to_all x0 -> x1, blocking collectives: none -> 24.9 us  [on_device(): lax.all_to_all(packed, 'dp', split_axis=0, concat_axis=0, tiled=True)]
    split x0 -> x6, local copies, waits for them, and re-layouts: none -> 13 us  [on_device(): jnp.split(triple, 3, axis=1)]
    reshape x1 -> x0, other arithmetic: 11.3 us -> none  [on_device(): recv_state.reshape(row_groups * capacity, local_heads, GROUP_DIMENSION, G...]
  transfers between devices with their start and end apart: 9 -> 7, of which waited for: 6 -> 5; matrix products, arithmetic and copies ran while one was open for 35% -> 30% of each run, Pallas kernels for 0% -> 0%
where the time goes in v1:
time: 553 us; the launch traced here: 546 us
  waiting for transfers between devices  279 us (50%)
  local copies, waits for them, and re-layouts  101 us (18%)
  matrix products  71.4 us (13%)
  other arithmetic  49.1 us (9%)
  blocking collectives  24.9 us (5%)
  between operations  14.9 us (3%)
    reduce_scatter x2, waiting for transfers between devices, summed(): lax.psum_scatter(values, 'dp', scatter_dimension=0, tiled=True)  132 us
    all_gather x1, waiting for transfers between devices, on_device(): chosen = lax.all_gather(own_chosen, ('dp', 'mp'), axis=0, tiled=True)  76.3 us
    all_gather x1, waiting for transfers between devices, on_device(): packed = lax.all_gather(packed, 'mp', axis=0, tiled=False)  42.4 us
    dot_general x7, matrix products, dot32(): return jnp.dot(left, right, preferred_element_type=jnp.float32)  40.3 us
    reduce_scatter x1, waiting for transfers between devices, on_device(): lax.psum_scatter(jnp.dot(hidden, out_cols, preferred_element_type=jnp.flo...  27.9 us
    all_to_all x1, blocking collectives, on_device(): lax.all_to_all(packed, 'dp', split_axis=0, concat_axis=0, tiled=True)  24.9 us
    unnamed x56, local copies, waits for them, and re-layouts  21.5 us
    reduce_sum x1, other arithmetic, wkv_blocks(): jnp.sum(acceptor_vectors[:, :, None] * lookup_vectors[:, None, :] * jnp.e...  13.1 us
  transfers between devices with their start and end apart: 7, of which 5 were waited for; matrix products, arithmetic and copies ran while one was open for 30% of the time, Pallas kernels for 0%

profile of v1, /device:TPU:0, one launch (start us, length us, event | category | flops | bytes accessed | tf_op | source)
XLA Modules:
  0.0 546.0 jit_solution(3768107224700433943)
XLA Ops:
  10.4 1.6 convert_subtract_fusion.1
  13.8 1.7 fusion.16
  16.5 24.9 %all_to_all.10 = bf16[4,82,1024]{2,1,0:T(8,128)(2,1)} all-to-all(bf16[4,82,1024]{2,1,0:T(8,128)(2,1)S(1)} %copy.145), channel_id=1, replica_groups=mesh['dp'=4,'mp'=8] {'dp'}, dimensions={0} | all-to-all | bytes 1343488 | tf_op jit(solution)/shard_map/all_to_all | solution.py:145
  41.6 42.4 %all-gather.8.cloned.1.call-done = bf16[32,82,1024]{2,1,0:T(8,128)(2,1)} async-done(((bf16[4,82,1024]{2,1,0:T(8,128)(2,1)}), bf16[32,82,1024]{2,1,0:T(8,128)(2,1)}) %all-gather.8.cloned.1.call-update) | async-done | bytes 5373968 | tf_op jit(solution)/shard_map/all_gather | solution.py:146
  84.0 3.3 copy.185
  87.9 2.5 slice.101
  90.9 1.7 reshape_reshape.7
  92.7 5.1 pad_maximum_fusion.1
  97.8 9.5 %convolution_convert_fusion.3 = bf16[2048,512]{0,1:T(8,128)(2,1)} fusion(bf16[1024,512]{1,0:T(8,128)(2,1)} %param.33, bf16[2048,1024]{1,0:T(8,128)(2,1)} %bitcast.130, bf16[2048,1024]{1,0:T(8,128)(2,1)} %bitcast.136, f32[1024]{0:T(1024)S(1)} %bitcast.151, bf16[2048,224]{1,0:T(8,128)(2,1)S(1)} %reshape_reshape.7, bf16[5,32,4096]{2,1,0:T(8,128)(2,1)} %param.27, ...), kind=kOutput, calls=%fused_computation.27 | convolution fusion | flops 2297430016 | bytes 12128264 | tf_op jit(solution)/shard_map/dot_general | solution.py:19
  107.3 9.6 %convolution_convert_fusion.2 = bf16[2048,512]{0,1:T(8,128)(2,1)} fusion(bf16[1024,512]{1,0:T(8,128)(2,1)} %param.34, bf16[2048,1024]{1,0:T(8,128)(2,1)} %bitcast.131, bf16[2048,1024]{1,0:T(8,128)(2,1)} %bitcast.137, f32[1024]{0:T(1024)S(1)} %bitcast.150, bf16[2048,224]{1,0:T(8,128)(2,1)S(1)} %reshape_reshape.7, bf16[5,32,4096]{2,1,0:T(8,128)(2,1)} %param.27, ...), kind=kOutput, calls=%fused_computation.26 | convolution fusion | flops 2297430016 | bytes 12128264 | tf_op jit(solution)/shard_map/dot_general | solution.py:19
  116.9 9.8 %convolution_convert_fusion.4 = bf16[2048,512]{0,1:T(8,128)(2,1)} fusion(bf16[1024,512]{1,0:T(8,128)(2,1)} %param.32, bf16[2048,1024]{1,0:T(8,128)(2,1)} %bitcast.132, bf16[2048,1024]{1,0:T(8,128)(2,1)} %bitcast.138, f32[1024]{0:T(1024)S(1)} %bitcast.149, bf16[2048,224]{1,0:T(8,128)(2,1)S(1)} %reshape_reshape.7, bf16[5,32,4096]{2,1,0:T(8,128)(2,1)} %param.27, ...), kind=kOutput, calls=%fused_computation.28 | convolution fusion | flops 2297430016 | bytes 12128264 | tf_op jit(solution)/shard_map/dot_general | solution.py:19
  126.7 5.8 %pad_maximum_fusion = bf16[2048,1536]{0,1:T(8,128)(2,1)} fusion(bf16[2048,512]{0,1:T(8,128)(2,1)} %convolution_convert_fusion.2, bf16[2048,512]{0,1:T(8,128)(2,1)} %convolution_convert_fusion.3, bf16[2048,512]{0,1:T(8,128)(2,1)} %convolution_convert_fusion.4), kind=kLoop, calls=%fused_computation.17 | loop fusion | flops 18874368 | bytes 12582912 | tf_op jit(solution)/shard_map/concatenate | solution.py:179
  133.4 8.8 %convolution_convert_fusion.1 = bf16[2048,512]{1,0:T(8,128)(2,1)} fusion(bf16[1024,512]{1,0:T(8,128)(2,1)} %param.35, bf16[2048,1024]{1,0:T(8,128)(2,1)} %bitcast.133, bf16[2048,1024]{1,0:T(8,128)(2,1)} %bitcast.139, f32[1024]{0:T(1024)S(1)} %bitcast.148, bf16[2048,224]{1,0:T(8,128)(2,1)S(1)} %reshape_reshape.7, bf16[5,32,4096]{2,1,0:T(8,128)(2,1)} %param.27, ...), kind=kOutput, calls=%fused_computation.25 | convolution fusion | flops 2297430016 | bytes 12128264 | tf_op jit(solution)/shard_map/dot_general | solution.py:19
  146.2 2.1 reshape.370
  148.7 1.8 reshape.371
  150.5 1.8 fusion.68
  152.3 1.6 concatenate.26
  153.9 2.2 gather_fusion.4
  156.9 86.6 %reduce-scatter.4.cloned.1.call-done = bf16[512,1536]{0,1:T(8,128)(2,1)} async-done(((bf16[2048,1536]{0,1:T(8,128)(2,1)}), bf16[512,1536]{0,1:T(8,128)(2,1)}) %reduce-scatter.4.cloned.1.call-update) | async-done | bytes 1572880 | tf_op jit(solution)/shard_map/reduce_scatter | solution.py:175
  245.5 1.6 reshape.372
  247.2 3.2 fusion.64
  250.4 2.6 copy.152
  252.9 2.8 mul.163
  255.7 2.6 copy.156
  258.3 2.7 reshape.373
  261.0 2.6 copy.149
  263.6 2.8 reshape.369
  266.4 6.2 %exponential_multiply_fusion = (f32[32,16,8,64]{3,2,1,0:T(8,128)}, f32[32,16,8,64]{3,2,1,0:T(8,128)}, f32[32,16,8]{2,1,0:T(8,128)S(1)}, f32[32,16,8,64]{3,2,1,0:T(8,128)S(1)}) fusion(f32[32,16,8,64]{3,2,1,0:T(8,128)} %mul.163, f32[32,16,8,64]{3,2,1,0:T(8,128)S(1)} %fusion.68, f32[32,8,64]{2,1,0:T(8,128)S(1)} %get-tuple-element.6, ...), kind=kLoop, calls=%fused_computation.35 | loop fusion | flops 1830912 | bytes 6375936 | tf_op jit(solution)/shard_map/mul | solution.py:64
  272.7 13.1 %multiply_reduce_fusion = f32[32,16,16,8]{3,2,1,0:T(8,128)} fusion(f32[32,16,8,64]{3,2,1,0:T(8,128)S(1)} %fusion.68, f32[32,16,8,64]{3,2,1,0:T(8,128)S(1)} %get-tuple-element.12, f32[32,16,8,64]{3,2,1,0:T(8,128)S(1)} %copy-done.4, f32[32,16,8,64]{3,2,1,0:T(8,128)S(1)} %copy-done.5, pred[16,16]{1,0:T(8,128)(4,1)S(1)} %iota_compare_fusion.3), kind=kLoop, calls=%fused_computation.6 | loop fusion | flops 20905984 | bytes 4456704 | tf_op jit(solution)/shard_map/reduce_sum | solution.py:52
  285.7 4.0 copy.154
  289.8 10.0 %fusion.9 = f32[32,8,16,64]{3,2,1,0:T(8,128)S(1)} fusion(f32[32,8,64,64]{3,2,1,0:T(8,128)} %param.23, f32[32,16,8,64]{3,2,1,0:T(8,128)S(1)} %copy-done.9), kind=kOutput, calls=%fused_computation.33 | convolution fusion | flops 201326592 | bytes 6291456 | tf_op jit(solution)/shard_map/bthi,bhij->bthj/dot_general | solution.py:43
  299.8 2.6 fusion.66
  303.5 2.2 copy.158
  307.1 2.7 reshape.374
  312.3 2.5 copy.161
  315.9 2.5 copy.165
  318.5 11.7 %add_convert_fusion = bf16[32,8,64,64]{3,2,1,0:T(8,128)(2,1)} fusion(f32[32,8,64,64]{3,2,1,0:T(8,128)} %param.23, f32[32,8,64]{2,1,0:T(8,128)S(1)} %copy-done.13, f32[32,16,8,64]{3,2,1,0:T(8,128)S(1)} %copy-done.8, bf16[32,16,8,64]{3,2,1,0:T(8,128)(2,1)S(1)} %reshape.372), kind=kOutput, calls=%fused_computation.16 | convolution fusion | flops 204472320 | bytes 7929856 | tf_op jit(solution)/shard_map/bshi,bshj->bhij/dot_general | solution.py:65
  330.2 7.8 %gather_fusion = bf16[64,8,64,64]{3,2,1,0:T(8,128)(2,1)} fusion(bf16[32,8,64,64]{3,2,1,0:T(8,128)(2,1)} %add_convert_fusion, s32[1024]{0:T(1024)S(1)} %pad_clamp_fusion.2), kind=kCustom, calls=%fused_computation | custom fusion | bytes 8388864 | tf_op jit(solution)/shard_map/gather | solution.py:253
  338.0 9.7 %reshape.439 = bf16[4,2,262144]{2,1,0:T(2,128)(2,1)} reshape(bf16[4,16,8,64,64]{4,3,2,1,0:T(8,128)(2,1)} %bitcast.122) | data formatting | bytes 8388608
  347.8 5.1 all-to-all-start.1
  353.0 45.1 %reduce-scatter.6.cloned.1.call-done = bf16[512,512]{1,0:T(8,128)(2,1)} async-done(((bf16[2048,512]{1,0:T(8,128)(2,1)}), bf16[512,512]{1,0:T(8,128)(2,1)}) %reduce-scatter.6.cloned.1.call-update) | async-done | bytes 524304 | tf_op jit(solution)/shard_map/reduce_scatter | solution.py:175
  398.1 6.8 %convolution_convert_fusion = bf16[512,4096]{1,0:T(8,128)(2,1)} fusion(bf16[512,4096]{1,0:T(8,128)(2,1)} %all-gather.6.cloned.1.call-done, bf16[512,512]{1,0:T(8,128)(2,1)} %reduce-scatter.6.cloned.1.call-done, f32[512,512]{1,0:T(8,128)S(1)} %copy-done.12, f32[512,512]{1,0:T(8,128)S(1)} %copy-done.10, f32[512,512]{1,0:T(8,128)S(1)} %copy-done.11, ...), kind=kOutput, calls=%fused_computation.18 | convolution fusion | flops 2152464384 | bytes 12062720 | tf_op jit(solution)/shard_map/dot_general | solution.py:217
  406.7 76.3 %all-gather.10.cloned.1.call-done = bf16[32,4,4096]{2,1,0:T(4,128)(2,1)} async-done(((bf16[1,4,4096]{2,1,0:T(4,128)(2,1)}), bf16[32,4,4096]{2,1,0:T(4,128)(2,1)}) %all-gather.10.cloned.1.call-update) | async-done | bytes 1048592 | tf_op jit(solution)/shard_map/all_gather | solution.py:236
  485.6 9.3 %reshape.440 = bf16[4,16,8,64,64]{4,3,2,1,0:T(8,128)(2,1)} reshape(bf16[4,2,262144]{2,1,0:T(2,128)(2,1)} %all-to-all-done.1) | data formatting | bytes 8388608
  494.9 7.3 %gather_fusion.2 = bf16[32,8,64,64]{3,2,1,0:T(8,128)(2,1)} fusion(bf16[64,8,64,64]{3,2,1,0:T(8,128)(2,1)} %bitcast.128, s32[1024]{0:T(1024)S(1)} %pad_clamp_fusion), kind=kCustom, calls=%fused_computation.2 | custom fusion | bytes 4194432 | tf_op jit(solution)/shard_map/gather | solution.py:260
  502.2 6.8 %convert_element_type.110 = f32[32,8,64,64]{3,2,1,0:T(8,128)} convert(bf16[32,8,64,64]{3,2,1,0:T(8,128)(2,1)} %gather_fusion.2) | non-fusion elementwise | flops 1048576 | bytes 6291456 | tf_op jit(solution)/shard_map/convert_element_type | solution.py:262
  509.0 27.9 %reduce-scatter.8.cloned.1.call-done = bf16[64,4096]{1,0:T(8,128)(2,1)} async-done(((bf16[512,4096]{1,0:T(8,128)(2,1)}), bf16[64,4096]{1,0:T(8,128)(2,1)}) %reduce-scatter.8.cloned.1.call-update) | async-done | bytes 524304 | tf_op jit(solution)/shard_map/reduce_scatter | solution.py:216
  536.9 2.1 fusion.22
  (138 shorter events, 25.5 us)
Async XLA Ops:
  7.2 6.1 %copy-start = (bf16[4096,160]{0,1:T(8,128)(2,1)S(1)}, bf16[4096,160]{0,1:T(8,128)(2,1)}, u32[]{:S(2)}) copy-start(bf16[4096,160]{0,1:T(8,128)(2,1)} %param.26) | copy-start | bytes 3932164
  7.2 6.6 %slice-start = ((f32[5,4096]{1,0:T(8,128)}), f32[1,4096]{1,0:T(1,128)S(1)}, s32[]{:S(2)}) async-start(f32[5,4096]{1,0:T(8,128)} %param.25), calls=%async_computation.11 | async-start | bytes 32768 | tf_op jit(solution)/shard_map/slice | solution.py:122
  7.2 6.6 %copy-start.2 = (bf16[4,16,4096]{2,1,0:T(8,128)(2,1)S(1)}, bf16[4,16,4096]{2,1,0:T(8,128)(2,1)}, u32[]{:S(2)}) copy-start(bf16[4,16,4096]{2,1,0:T(8,128)(2,1)} %param.21) | copy-start | bytes 1572868
  7.2 76.8 %all-gather.8.cloned.1.call-start = ((), (), s32[]{:S(2)}) async-start(), calls=%async_computation.9 | async-start | bytes 6488064 | tf_op jit(solution)/shard_map/all_gather | solution.py:146
  13.8 27.7 %copy-start.15 = (f32[5,4096]{1,0:T(8,128)S(1)}, f32[5,4096]{1,0:T(8,128)}, u32[]{:S(2)}) copy-start(f32[5,4096]{1,0:T(8,128)} %param.25) | copy-start | bytes 245764
  41.4 202.0 %reduce-scatter.4.cloned.1.call-start = ((), (), s32[]{:S(2)}) async-start(), calls=%async_computation.5 | async-start | bytes 7864320 | tf_op jit(solution)/shard_map/reduce_scatter | solution.py:175
  132.6 220.4 %all-gather.6.cloned.1.call-start = ((), (), s32[]{:S(2)}) async-start(), calls=%async_computation.7 | async-start | bytes 5242880 | tf_op jit(solution)/shard_map/all_gather | solution.py:215
  133.3 264.8 %reduce-scatter.6.cloned.1.call-start = ((), (), s32[]{:S(2)}) async-start(), calls=%async_computation.6 | async-start | bytes 2621440 | tf_op jit(solution)/shard_map/reduce_scatter | solution.py:175
  133.3 9.4 %copy-start.19 = (s32[128]{0:T(128)S(1)}, s32[128]{0:T(128)}, u32[]{:S(2)}) copy-start(s32[128]{0:T(128)} %param.40) | copy-start | bytes 1540
  133.4 9.5 %copy-start.14 = (bf16[4,4096]{1,0:T(4,128)(2,1)S(1)}, bf16[4,4096]{1,0:T(4,128)(2,1)}, u32[]{:S(2)}) copy-start(bf16[4,4096]{1,0:T(4,128)(2,1)} %param.22) | copy-start | bytes 98308
  142.2 3.1 copy-start.23
  142.2 6.2 %copy-start.16 = (bf16[64,512]{1,0:T(8,128)(2,1)S(1)}, bf16[64,512]{1,0:T(8,128)(2,1)}, u32[]{:S(2)}) copy-start(bf16[64,512]{1,0:T(8,128)(2,1)} %param.30) | copy-start | bytes 196612
  142.2 6.2 %copy-start.17 = (f32[512]{0:T(512)S(1)}, f32[512]{0:T(512)}, u32[]{:S(2)}) copy-start(f32[512]{0:T(512)} %param.28) | copy-start | bytes 6148
  142.2 340.8 %all-gather.10.cloned.1.call-start = ((), (), s32[]{:S(2)}) async-start(), calls=%async_computation.10 | async-start | bytes 1081344 | tf_op jit(solution)/shard_map/all_gather | solution.py:236
  150.5 5.6 %copy-start.18 = (pred[32]{0:T(512)(128)(4,1)S(1)}, pred[32]{0:T(512)(128)(4,1)}, u32[]{:S(2)}) copy-start(pred[32]{0:T(512)(128)(4,1)} %get-tuple-element.7) | copy-start | bytes 100
  266.4 6.2 %copy-start.4 = (f32[32,16,8,64]{3,2,1,0:T(8,128)S(1)}, f32[32,16,8,64]{3,2,1,0:T(8,128)}, u32[]{:S(2)}) copy-start(f32[32,16,8,64]{3,2,1,0:T(8,128)} %mul.163) | copy-start | bytes 3145732
  266.4 6.2 %copy-start.5 = (f32[32,16,8,64]{3,2,1,0:T(8,128)S(1)}, f32[32,16,8,64]{3,2,1,0:T(8,128)}, u32[]{:S(2)}) copy-start(f32[32,16,8,64]{3,2,1,0:T(8,128)} %reshape.369) | copy-start | bytes 3145732
  285.7 4.1 copy-start.9
  289.8 10.0 %copy-start.6 = (f32[32,16,16,8]{2,1,3,0:T(8,128)S(1)}, f32[32,16,16,8]{2,1,3,0:T(8,128)}, u32[]{:S(2)}) copy-start(f32[32,16,16,8]{2,1,3,0:T(8,128)} %copy.154) | copy-start | bytes 786436
  289.8 10.0 %copy-start.7 = (f32[32,16,8,64]{3,2,1,0:T(8,128)S(1)}, f32[32,16,8,64]{3,2,1,0:T(8,128)}, u32[]{:S(2)}) copy-start(f32[32,16,8,64]{3,2,1,0:T(8,128)} %reshape.373) | copy-start | bytes 3145732
  309.8 8.7 %copy-start.8 = (f32[32,16,8,64]{3,2,1,0:T(8,128)S(1)}, f32[32,16,8,64]{3,2,1,0:T(8,128)}, u32[]{:S(2)}) copy-start(f32[32,16,8,64]{3,2,1,0:T(8,128)} %get-tuple-element.9) | copy-start | bytes 3145732
  309.8 8.7 %copy-start.13 = (f32[32,8,64]{2,1,0:T(8,128)S(1)}, f32[32,8,64]{2,1,0:T(8,128)}, u32[]{:S(2)}) copy-start(f32[32,8,64]{2,1,0:T(8,128)} %get-tuple-element.5) | copy-start | bytes 196612
  347.8 50.3 %copy-start.10 = (f32[512,512]{1,0:T(8,128)S(1)}, f32[512,512]{1,0:T(8,128)}, u32[]{:S(2)}) copy-start(f32[512,512]{1,0:T(8,128)} %reshape.374) | copy-start | bytes 3145732
  347.8 50.3 %copy-start.11 = (f32[512,512]{1,0:T(8,128)S(1)}, f32[512,512]{1,0:T(8,128)}, u32[]{:S(2)}) copy-start(f32[512,512]{1,0:T(8,128)} %copy.161) | copy-start | bytes 3145732
  347.8 50.3 %copy-start.12 = (f32[512,512]{1,0:T(8,128)S(1)}, f32[512,512]{1,0:T(8,128)}, u32[]{:S(2)}) copy-start(f32[512,512]{1,0:T(8,128)} %copy.165) | copy-start | bytes 3145732
  347.8 50.3 %copy-start.20 = (f32[512]{0:T(512)S(1)}, f32[512]{0:T(512)}, u32[]{:S(2)}) copy-start(f32[512]{0:T(512)} %param.38) | copy-start | bytes 6148
  347.8 50.3 %copy-start.21 = (f32[512]{0:T(512)S(1)}, f32[512]{0:T(512)}, u32[]{:S(2)}) copy-start(f32[512]{0:T(512)} %param.37) | copy-start | bytes 6148
  347.8 137.8 %all-to-all-start.1 = ((bf16[4,2,262144]{2,1,0:T(2,128)(2,1)}), bf16[4,2,262144]{2,1,0:T(2,128)(2,1)}, u32[]{:S(2)}, u32[]{:S(2)}) async-start(bf16[4,2,262144]{2,1,0:T(2,128)(2,1)} %reshape.439), calls=%async_computation.4 | async-start | bytes 8388608 | tf_op jit(solution)/shard_map/all_to_all | solution.py:254
  352.9 184.0 %reduce-scatter.8.cloned.1.call-start = ((), (), s32[]{:S(2)}) async-start(), calls=%async_computation.8 | async-start | bytes 4718592 | tf_op jit(solution)/shard_map/reduce_scatter | solution.py:216
  404.9 0.7 copy-start.22
  404.9 0.7 copy-start.24
  494.9 44.0 %copy-start.1 = (bf16[4096,160]{0,1:T(8,128)(2,1)S(1)}, bf16[4096,160]{0,1:T(8,128)(2,1)}, u32[]{:S(2)}) copy-start(bf16[4096,160]{0,1:T(8,128)(2,1)} %param.26) | copy-start | bytes 3932164
  502.2 34.7 %copy-start.3 = (bf16[4,16,4096]{2,1,0:T(8,128)(2,1)S(1)}, bf16[4,16,4096]{2,1,0:T(8,128)(2,1)}, u32[]{:S(2)}) copy-start(bf16[4,16,4096]{2,1,0:T(8,128)(2,1)} %param.21) | copy-start | bytes 1572868
Sparse Core Ops, SparseCore 0:
  41.5 42.4 all-gather.7
  132.7 110.7 reduce-scatter.3
  245.0 81.2 all-gather.5
  328.5 69.5 reduce-scatter.5
  401.8 81.1 all-gather.9
  486.6 50.2 reduce-scatter.7

commit v2 on v1

--- a/solution.py
+++ b/solution.py
@@ -186,7 +186,10 @@
         )
     )
     acceptor_vectors, lookup_vectors, payload_vectors = jnp.split(triple, 3, axis=1)
-    gate_raw = summed(partial(4, gating_matrix))
+    gate_summed = lax.psum_scatter(
+        partial(4, gating_matrix), "dp", scatter_dimension=0, tiled=True
+    )
+    gate_raw = gate_summed.astype(jnp.float32)
     row_narrow = lax.dynamic_index_in_dim(narrow, row_index, 0, keepdims=False)
     decay_inner_rows = row_narrow[:, narrow_width - decay_width :]
     logarithmic_fading_entries = -jnp.exp(
@@ -212,6 +215,7 @@
         groupwise_scaling_factor,
         groupwise_scaling_offset,
     )
+    emission_matrix, gate_summed = lax.optimization_barrier((emission_matrix, gate_summed))
     out_cols = lax.all_gather(emission_matrix, "dp", axis=1, tiled=True)
     attended = lax.psum_scatter(
         jnp.dot(hidden, out_cols, preferred_element_type=jnp.float32).astype(jnp.bfloat16),
@@ -233,8 +237,13 @@
     own_accepted = lax.dynamic_slice_in_dim(approved_guesses, own_start, own_reqs)
     edge_rows = jnp.concatenate([preceding_symbol_vector[:, None, :], guess_vectors], axis=1)
     own_chosen = jnp.take_along_axis(edge_rows, own_accepted[:, None, None], axis=1)[:, 0]
-    chosen = lax.all_gather(own_chosen, ("dp", "mp"), axis=0, tiled=True)
-    chosen_cols = lax.dynamic_slice_in_dim(chosen, group_index * local_width, local_width, 1)
+    row_chosen = lax.all_gather(own_chosen, "mp", axis=0, tiled=True)
+    chosen_cols = lax.all_gather(
+        lax.dynamic_slice_in_dim(row_chosen, group_index * local_width, local_width, 1),
+        "dp",
+        axis=0,
+        tiled=True,
+    )
     capacity = 2 * row_reqs // row_groups
     target_rows = (destination_slot // row_reqs).reshape(row_groups, row_reqs)
     onehot = (

time: 553 us -> 515 us (0.931)
  waiting for transfers between devices: 279 us -> 153 us
  blocking collectives: 24.9 us -> 114 us
    all_gather x0 -> x2, blocking collectives: none -> 89.1 us  [the longest x1 79.8 us: on_device(): lax.all_gather(lax.dynamic_slice_in_dim(row_chosen, group_index * local_w...]
    all_gather x1 -> x0, waiting for transfers between devices: 76.3 us -> none  [on_device(): chosen = lax.all_gather(own_chosen, ('dp', 'mp'), axis=0, tiled=True)]
    reduce_scatter x2 -> x1, waiting for transfers between devices: 132 us -> 102 us  [summed(): lax.psum_scatter(values, 'dp', scatter_dimension=0, tiled=True)]
    reduce_scatter x1, waiting for transfers between devices: 27.9 us -> 0.01 us  [on_device(): lax.psum_scatter(jnp.dot(hidden, out_cols, preferred_element_type=jnp.flo...]
    reduce_scatter x0 -> x1, waiting for transfers between devices: none -> 7.9 us  [on_device(): lax.psum_scatter(partial(4, gating_matrix), 'dp', scatter_dimension=0, ti...]
    unnamed x56 -> x60, local copies, waits for them, and re-layouts: 21.5 us -> 21.1 us
  transfers between devices with their start and end apart: 7 -> 6, of which waited for: 5 -> 3; matrix products, arithmetic and copies ran while one was open for 30% -> 36% of each run, Pallas kernels for 0% -> 0%
where the time goes in v2:
time: 515 us; the launch traced here: 506 us
  waiting for transfers between devices  153 us (30%)
  blocking collectives  114 us (22%)
  local copies, waits for them, and re-layouts  100 us (19%)
  matrix products  70.7 us (14%)
  other arithmetic  48.1 us (9%)
  between operations  14.9 us (3%)
  starting transfers between devices  5.79 us (1%)
    reduce_scatter x1, waiting for transfers between devices, summed(): lax.psum_scatter(values, 'dp', scatter_dimension=0, tiled=True)  102 us
    all_gather x1, blocking collectives, on_device(): lax.all_gather(lax.dynamic_slice_in_dim(row_chosen, group_index * local_w...  79.8 us
    all_gather x1, waiting for transfers between devices, on_device(): packed = lax.all_gather(packed, 'mp', axis=0, tiled=False)  42.4 us
    dot_general x7, matrix products, dot32(): return jnp.dot(left, right, preferred_element_type=jnp.float32)  39.5 us
    all_to_all x1, blocking collectives, on_device(): lax.all_to_all(packed, 'dp', split_axis=0, concat_axis=0, tiled=True)  24.9 us
    unnamed x60, local copies, waits for them, and re-layouts  21.1 us
    reduce_sum x1, other arithmetic, wkv_blocks(): jnp.sum(acceptor_vectors[:, :, None] * lookup_vectors[:, None, :] * jnp.e...  13.1 us
    split x6, local copies, waits for them, and re-layouts, on_device(): jnp.split(triple, 3, axis=1)  13 us
  transfers between devices with their start and end apart: 6, of which 3 were waited for; matrix products, arithmetic and copies ran while one was open for 36% of the time, Pallas kernels for 0%

profile of v2, /device:TPU:0, one launch (start us, length us, event | category | flops | bytes accessed | tf_op | source)
XLA Modules:
  0.0 506.3 jit_solution(15457518247251489341)
XLA Ops:
  10.4 1.6 convert_subtract_fusion.1
  13.8 1.7 fusion.16
  16.5 24.9 %all_to_all.10 = bf16[4,82,1024]{2,1,0:T(8,128)(2,1)} all-to-all(bf16[4,82,1024]{2,1,0:T(8,128)(2,1)S(1)} %copy.145), channel_id=1, replica_groups=mesh['dp'=4,'mp'=8] {'dp'}, dimensions={0} | all-to-all | bytes 1343488 | tf_op jit(solution)/shard_map/all_to_all | solution.py:145
  41.6 42.4 %all-gather.7.cloned.1.call-done = bf16[32,82,1024]{2,1,0:T(8,128)(2,1)} async-done(((bf16[4,82,1024]{2,1,0:T(8,128)(2,1)}), bf16[32,82,1024]{2,1,0:T(8,128)(2,1)}) %all-gather.7.cloned.1.call-update) | async-done | bytes 5373968 | tf_op jit(solution)/shard_map/all_gather | solution.py:146
  84.0 3.3 copy.185
  87.9 2.5 slice.101
  90.9 1.7 reshape_reshape.7
  92.7 5.3 %pad_maximum_fusion.1 = bf16[4,8,4,16,1024]{4,3,2,1,0:T(8,128)(2,1)} fusion(bf16[4,8,4,15,1024]{4,3,2,1,0:T(8,128)(2,1)} %bitcast.129, bf16[4,8,4,1,1024]{4,3,2,1,0:T(2,128)(2,1)S(1)} %copy.148), kind=kLoop, calls=%fused_computation.24 | loop fusion | flops 8388608 | bytes 8388608 | tf_op jit(solution)/shard_map/concatenate | solution.py:13
  98.0 8.8 %convolution_convert_fusion.1 = bf16[2048,512]{1,0:T(8,128)(2,1)} fusion(bf16[1024,512]{1,0:T(8,128)(2,1)} %param.35, bf16[2048,1024]{1,0:T(8,128)(2,1)} %bitcast.130, bf16[2048,1024]{1,0:T(8,128)(2,1)} %bitcast.136, f32[1024]{0:T(1024)S(1)} %bitcast.151, bf16[2048,224]{1,0:T(8,128)(2,1)S(1)} %reshape_reshape.7, bf16[5,32,4096]{2,1,0:T(8,128)(2,1)} %param.27, ...), kind=kOutput, calls=%fused_computation.25 | convolution fusion | flops 2297430016 | bytes 12128264 | tf_op jit(solution)/shard_map/dot_general | solution.py:19
  107.4 8.4 %convolution_convert_fusion.3 = bf16[2048,512]{0,1:T(8,128)(2,1)S(1)} fusion(bf16[1024,512]{1,0:T(8,128)(2,1)} %param.33, bf16[2048,1024]{1,0:T(8,128)(2,1)} %bitcast.131, bf16[2048,1024]{1,0:T(8,128)(2,1)} %bitcast.137, f32[1024]{0:T(1024)S(1)} %bitcast.150, bf16[2048,224]{1,0:T(8,128)(2,1)} %copy-done.12, bf16[5,32,4096]{2,1,0:T(8,128)(2,1)} %param.27, ...), kind=kOutput, calls=%fused_computation.27 | convolution fusion | flops 2297430016 | bytes 12128264 | tf_op jit(solution)/shard_map/dot_general | solution.py:19
  115.8 9.7 %convolution_convert_fusion.2 = bf16[2048,512]{0,1:T(8,128)(2,1)} fusion(bf16[1024,512]{1,0:T(8,128)(2,1)} %param.34, bf16[2048,1024]{1,0:T(8,128)(2,1)} %bitcast.132, bf16[2048,1024]{1,0:T(8,128)(2,1)} %bitcast.138, f32[1024]{0:T(1024)S(1)} %bitcast.149, bf16[2048,224]{1,0:T(8,128)(2,1)} %copy-done.12, bf16[5,32,4096]{2,1,0:T(8,128)(2,1)} %param.27, ...), kind=kOutput, calls=%fused_computation.26 | convolution fusion | flops 2297430016 | bytes 12128264 | tf_op jit(solution)/shard_map/dot_general | solution.py:19
  125.6 10.0 %convolution_convert_fusion.4 = bf16[2048,512]{0,1:T(8,128)(2,1)} fusion(bf16[1024,512]{1,0:T(8,128)(2,1)} %param.32, bf16[2048,1024]{1,0:T(8,128)(2,1)} %bitcast.133, bf16[2048,1024]{1,0:T(8,128)(2,1)} %bitcast.139, f32[1024]{0:T(1024)S(1)} %bitcast.148, bf16[2048,224]{1,0:T(8,128)(2,1)} %copy-done.12, bf16[5,32,4096]{2,1,0:T(8,128)(2,1)} %param.27, ...), kind=kOutput, calls=%fused_computation.28 | convolution fusion | flops 2297430016 | bytes 12128264 | tf_op jit(solution)/shard_map/dot_general | solution.py:19
  135.5 5.4 %pad_maximum_fusion = bf16[2048,1536]{0,1:T(8,128)(2,1)} fusion(bf16[2048,512]{0,1:T(8,128)(2,1)} %convolution_convert_fusion.2, bf16[2048,512]{0,1:T(8,128)(2,1)S(1)} %convolution_convert_fusion.3, bf16[2048,512]{0,1:T(8,128)(2,1)} %convolution_convert_fusion.4), kind=kLoop, calls=%fused_computation.17 | loop fusion | flops 18874368 | bytes 12582912 | tf_op jit(solution)/shard_map/concatenate | solution.py:179
  143.0 7.9 %reduce-scatter.6.cloned.1.call-done = bf16[512,512]{1,0:T(8,128)(2,1)} async-done(((bf16[2048,512]{1,0:T(8,128)(2,1)}), bf16[512,512]{1,0:T(8,128)(2,1)}) %reduce-scatter.6.cloned.1.call-update) | async-done | bytes 524304 | tf_op jit(solution)/shard_map/reduce_scatter | solution.py:189
  151.0 1.7 reshape.370
  153.2 1.8 reshape.371
  155.0 1.7 fusion.68
  156.7 1.6 concatenate.26
  158.3 2.9 gather_fusion.4
  161.9 102.1 %reduce-scatter.4.cloned.1.call-done = bf16[512,1536]{0,1:T(8,128)(2,1)} async-done(((bf16[2048,1536]{0,1:T(8,128)(2,1)}), bf16[512,1536]{0,1:T(8,128)(2,1)}) %reduce-scatter.4.cloned.1.call-update) | async-done | bytes 1572880 | tf_op jit(solution)/shard_map/reduce_scatter | solution.py:175
  266.1 1.6 reshape.372
  267.8 3.2 fusion.64
  271.0 2.6 copy.152
  273.6 2.8 mul.163
  276.4 2.5 copy.156
  278.9 2.8 reshape.373
  281.7 2.6 copy.149
  284.2 2.8 reshape.369
  287.0 6.2 %exponential_multiply_fusion = (f32[32,16,8,64]{3,2,1,0:T(8,128)}, f32[32,16,8,64]{3,2,1,0:T(8,128)}, f32[32,16,8]{2,1,0:T(8,128)S(1)}, f32[32,16,8,64]{3,2,1,0:T(8,128)S(1)}) fusion(f32[32,16,8,64]{3,2,1,0:T(8,128)} %mul.163, f32[32,16,8,64]{3,2,1,0:T(8,128)S(1)} %fusion.68, f32[32,8,64]{2,1,0:T(8,128)S(1)} %get-tuple-element.8, ...), kind=kLoop, calls=%fused_computation.35 | loop fusion | flops 1830912 | bytes 6375936 | tf_op jit(solution)/shard_map/mul | solution.py:64
  293.2 13.1 %multiply_reduce_fusion = f32[32,16,16,8]{3,2,1,0:T(8,128)} fusion(f32[32,16,8,64]{3,2,1,0:T(8,128)S(1)} %fusion.68, f32[32,16,8,64]{3,2,1,0:T(8,128)S(1)} %get-tuple-element.14, f32[32,16,8,64]{3,2,1,0:T(8,128)S(1)} %copy-done.4, f32[32,16,8,64]{3,2,1,0:T(8,128)S(1)} %copy-done.5, pred[16,16]{1,0:T(8,128)(4,1)S(1)} %iota_compare_fusion.3), kind=kLoop, calls=%fused_computation.6 | loop fusion | flops 20905984 | bytes 4456704 | tf_op jit(solution)/shard_map/reduce_sum | solution.py:52
  306.3 4.0 copy.154
  310.4 10.0 %fusion.9 = f32[32,8,16,64]{3,2,1,0:T(8,128)S(1)} fusion(f32[32,8,64,64]{3,2,1,0:T(8,128)} %param.23, f32[32,16,8,64]{3,2,1,0:T(8,128)S(1)} %copy-done.9), kind=kOutput, calls=%fused_computation.33 | convolution fusion | flops 201326592 | bytes 6291456 | tf_op jit(solution)/shard_map/bthi,bhij->bthj/dot_general | solution.py:43
  320.4 2.6 fusion.66
  324.1 2.2 copy.158
  327.8 2.7 reshape.374
  332.9 2.5 copy.161
  336.6 2.6 copy.165
  339.2 11.7 %add_convert_fusion = bf16[32,8,64,64]{3,2,1,0:T(8,128)(2,1)} fusion(f32[32,8,64,64]{3,2,1,0:T(8,128)} %param.23, f32[32,8,64]{2,1,0:T(8,128)S(1)} %copy-done.14, f32[32,16,8,64]{3,2,1,0:T(8,128)S(1)} %copy-done.8, bf16[32,16,8,64]{3,2,1,0:T(8,128)(2,1)S(1)} %reshape.372), kind=kOutput, calls=%fused_computation.16 | convolution fusion | flops 204472320 | bytes 7929856 | tf_op jit(solution)/shard_map/bshi,bshj->bhij/dot_general | solution.py:65
  350.9 7.8 %gather_fusion = bf16[64,8,64,64]{3,2,1,0:T(8,128)(2,1)} fusion(bf16[32,8,64,64]{3,2,1,0:T(8,128)(2,1)} %add_convert_fusion, s32[1024]{0:T(1024)S(1)} %pad_clamp_fusion.2), kind=kCustom, calls=%fused_computation | custom fusion | bytes 8388864 | tf_op jit(solution)/shard_map/gather | solution.py:262
  358.7 9.8 %reshape.439 = bf16[4,2,262144]{2,1,0:T(2,128)(2,1)} reshape(bf16[4,16,8,64,64]{4,3,2,1,0:T(8,128)(2,1)} %bitcast.122) | data formatting | bytes 8388608
  368.5 5.1 %all-to-all-start.1 = ((bf16[4,2,262144]{2,1,0:T(2,128)(2,1)}), bf16[4,2,262144]{2,1,0:T(2,128)(2,1)}, u32[]{:S(2)}, u32[]{:S(2)}) async-start(bf16[4,2,262144]{2,1,0:T(2,128)(2,1)} %reshape.439), calls=%async_computation.4 | async-start | bytes 8388608 | tf_op jit(solution)/shard_map/all_to_all | solution.py:263
  373.7 6.8 %convolution_convert_fusion = bf16[512,4096]{1,0:T(8,128)(2,1)} fusion(bf16[512,4096]{1,0:T(8,128)(2,1)} %all-gather.5.cloned.1.call-done, bf16[512,512]{1,0:T(8,128)(2,1)} %reduce-scatter.6.cloned.1.call-done, f32[512,512]{1,0:T(8,128)S(1)} %copy-done.13, f32[512,512]{1,0:T(8,128)S(1)} %copy-done.10, f32[512,512]{1,0:T(8,128)S(1)} %copy-done.11, ...), kind=kOutput, calls=%fused_computation.18 | convolution fusion | flops 2152464384 | bytes 12062720 | tf_op jit(solution)/shard_map/dot_general | solution.py:221
  383.4 9.3 %all-gather.1 = bf16[8,4,4096]{2,1,0:T(4,128)(2,1)S(1)} all-gather(bf16[1,4,4096]{2,1,0:T(4,128)(2,1)S(1)} %select_bitcast_fusion), channel_id=1, replica_groups=mesh['dp'=4,'mp'=8] {'mp'}, dimensions={0}, use_global_device_ids=true | all-gather | bytes 294912 | tf_op jit(solution)/shard_map/all_gather | solution.py:240
  393.7 79.8 %all_gather.19 = bf16[128,512]{1,0:T(8,128)(2,1)S(1)} all-gather(bf16[32,512]{1,0:T(8,128)(2,1)S(1)} %constant_dynamic-slice_fusion), channel_id=1, replica_groups=mesh['dp'=4,'mp'=8] {'dp'}, dimensions={0}, use_global_device_ids=true | all-gather | bytes 163840 | tf_op jit(solution)/shard_map/all_gather | solution.py:241
  474.8 9.3 %reshape.440 = bf16[4,16,8,64,64]{4,3,2,1,0:T(8,128)(2,1)} reshape(bf16[4,2,262144]{2,1,0:T(2,128)(2,1)} %all-to-all-done.1) | data formatting | bytes 8388608
  484.1 6.5 %gather_fusion.2 = bf16[32,8,64,64]{3,2,1,0:T(8,128)(2,1)} fusion(bf16[64,8,64,64]{3,2,1,0:T(8,128)(2,1)} %bitcast.128, s32[1024]{0:T(1024)S(1)} %pad_clamp_fusion), kind=kCustom, calls=%fused_computation.2 | custom fusion | bytes 4194432 | tf_op jit(solution)/shard_map/gather | solution.py:269
  490.6 6.7 %convert_element_type.110 = f32[32,8,64,64]{3,2,1,0:T(8,128)} convert(bf16[32,8,64,64]{3,2,1,0:T(8,128)(2,1)} %gather_fusion.2) | non-fusion elementwise | flops 1048576 | bytes 6291456 | tf_op jit(solution)/shard_map/convert_element_type | solution.py:271
  497.3 2.1 fusion.22
  (141 shorter events, 24.3 us)
Async XLA Ops:
  7.2 6.1 %copy-start = (bf16[4096,160]{0,1:T(8,128)(2,1)S(1)}, bf16[4096,160]{0,1:T(8,128)(2,1)}, u32[]{:S(2)}) copy-start(bf16[4096,160]{0,1:T(8,128)(2,1)} %param.26) | copy-start | bytes 3932164
  7.2 6.6 %slice-start = ((f32[5,4096]{1,0:T(8,128)}), f32[1,4096]{1,0:T(1,128)S(1)}, s32[]{:S(2)}) async-start(f32[5,4096]{1,0:T(8,128)} %param.25), calls=%async_computation.10 | async-start | bytes 32768 | tf_op jit(solution)/shard_map/slice | solution.py:122
  7.2 6.6 %copy-start.2 = (bf16[4,16,4096]{2,1,0:T(8,128)(2,1)S(1)}, bf16[4,16,4096]{2,1,0:T(8,128)(2,1)}, u32[]{:S(2)}) copy-start(bf16[4,16,4096]{2,1,0:T(8,128)(2,1)} %param.21) | copy-start | bytes 1572868
  7.2 76.8 %all-gather.7.cloned.1.call-start = ((), (), s32[]{:S(2)}) async-start(), calls=%async_computation.9 | async-start | bytes 6488064 | tf_op jit(solution)/shard_map/all_gather | solution.py:146
  13.8 27.7 %copy-start.16 = (f32[5,4096]{1,0:T(8,128)S(1)}, f32[5,4096]{1,0:T(8,128)}, u32[]{:S(2)}) copy-start(f32[5,4096]{1,0:T(8,128)} %param.25) | copy-start | bytes 245764
  41.4 109.5 %reduce-scatter.6.cloned.1.call-start = ((), (), s32[]{:S(2)}) async-start(), calls=%async_computation.6 | async-start | bytes 2621440 | tf_op jit(solution)/shard_map/reduce_scatter | solution.py:189
  92.7 5.3 %copy-start.12 = (bf16[2048,224]{1,0:T(8,128)(2,1)}, bf16[2048,224]{1,0:T(8,128)(2,1)S(1)}, u32[]{:S(2)}) copy-start(bf16[2048,224]{1,0:T(8,128)(2,1)S(1)} %reshape_reshape.7) | copy-start | bytes 2752516
  106.9 157.1 %reduce-scatter.4.cloned.1.call-start = ((), (), s32[]{:S(2)}) async-start(), calls=%async_computation.5 | async-start | bytes 7864320 | tf_op jit(solution)/shard_map/reduce_scatter | solution.py:175
  140.9 0.7 copy-start.25
  140.9 1.4 copy-start.20
  140.9 11.9 %copy-start.17 = (bf16[64,512]{1,0:T(8,128)(2,1)S(1)}, bf16[64,512]{1,0:T(8,128)(2,1)}, u32[]{:S(2)}) copy-start(bf16[64,512]{1,0:T(8,128)(2,1)} %param.30) | copy-start | bytes 196612
  140.9 11.9 %copy-start.18 = (f32[512]{0:T(512)S(1)}, f32[512]{0:T(512)}, u32[]{:S(2)}) copy-start(f32[512]{0:T(512)} %param.28) | copy-start | bytes 6148
  141.0 232.7 %all-gather.5.cloned.1.call-start = ((), (), s32[]{:S(2)}) async-start(), calls=%async_computation.7 | async-start | bytes 5242880 | tf_op jit(solution)/shard_map/all_gather | solution.py:219
  154.9 6.2 %copy-start.19 = (pred[32]{0:T(512)(128)(4,1)S(1)}, pred[32]{0:T(512)(128)(4,1)}, u32[]{:S(2)}) copy-start(pred[32]{0:T(512)(128)(4,1)} %get-tuple-element.9) | copy-start | bytes 100
  287.0 6.2 %copy-start.4 = (f32[32,16,8,64]{3,2,1,0:T(8,128)S(1)}, f32[32,16,8,64]{3,2,1,0:T(8,128)}, u32[]{:S(2)}) copy-start(f32[32,16,8,64]{3,2,1,0:T(8,128)} %mul.163) | copy-start | bytes 3145732
  287.0 6.2 %copy-start.5 = (f32[32,16,8,64]{3,2,1,0:T(8,128)S(1)}, f32[32,16,8,64]{3,2,1,0:T(8,128)}, u32[]{:S(2)}) copy-start(f32[32,16,8,64]{3,2,1,0:T(8,128)} %reshape.369) | copy-start | bytes 3145732
  306.3 4.1 copy-start.9
  310.4 10.0 %copy-start.6 = (f32[32,16,16,8]{2,1,3,0:T(8,128)S(1)}, f32[32,16,16,8]{2,1,3,0:T(8,128)}, u32[]{:S(2)}) copy-start(f32[32,16,16,8]{2,1,3,0:T(8,128)} %copy.154) | copy-start | bytes 786436
  310.4 10.0 %copy-start.7 = (f32[32,16,8,64]{3,2,1,0:T(8,128)S(1)}, f32[32,16,8,64]{3,2,1,0:T(8,128)}, u32[]{:S(2)}) copy-start(f32[32,16,8,64]{3,2,1,0:T(8,128)} %reshape.373) | copy-start | bytes 3145732
  330.5 8.7 %copy-start.8 = (f32[32,16,8,64]{3,2,1,0:T(8,128)S(1)}, f32[32,16,8,64]{3,2,1,0:T(8,128)}, u32[]{:S(2)}) copy-start(f32[32,16,8,64]{3,2,1,0:T(8,128)} %get-tuple-element.11) | copy-start | bytes 3145732
  330.5 8.7 %copy-start.14 = (f32[32,8,64]{2,1,0:T(8,128)S(1)}, f32[32,8,64]{2,1,0:T(8,128)}, u32[]{:S(2)}) copy-start(f32[32,8,64]{2,1,0:T(8,128)} %get-tuple-element.7) | copy-start | bytes 196612
  368.5 5.2 %copy-start.10 = (f32[512,512]{1,0:T(8,128)S(1)}, f32[512,512]{1,0:T(8,128)}, u32[]{:S(2)}) copy-start(f32[512,512]{1,0:T(8,128)} %reshape.374) | copy-start | bytes 3145732
  368.5 5.2 %copy-start.11 = (f32[512,512]{1,0:T(8,128)S(1)}, f32[512,512]{1,0:T(8,128)}, u32[]{:S(2)}) copy-start(f32[512,512]{1,0:T(8,128)} %copy.161) | copy-start | bytes 3145732
  368.5 5.2 %copy-start.13 = (f32[512,512]{1,0:T(8,128)S(1)}, f32[512,512]{1,0:T(8,128)}, u32[]{:S(2)}) copy-start(f32[512,512]{1,0:T(8,128)} %copy.165) | copy-start | bytes 3145732
  368.5 5.3 %copy-start.22 = (f32[512]{0:T(512)S(1)}, f32[512]{0:T(512)}, u32[]{:S(2)}) copy-start(f32[512]{0:T(512)} %param.38) | copy-start | bytes 6148
  368.5 5.3 %copy-start.23 = (f32[512]{0:T(512)S(1)}, f32[512]{0:T(512)}, u32[]{:S(2)}) copy-start(f32[512]{0:T(512)} %param.37) | copy-start | bytes 6148
  368.5 106.3 %all-to-all-start.1 = ((bf16[4,2,262144]{2,1,0:T(2,128)(2,1)}), bf16[4,2,262144]{2,1,0:T(2,128)(2,1)}, u32[]{:S(2)}, u32[]{:S(2)}) async-start(bf16[4,2,262144]{2,1,0:T(2,128)(2,1)} %reshape.439), calls=%async_computation.4 | async-start | bytes 8388608 | tf_op jit(solution)/shard_map/all_to_all | solution.py:263
  373.6 123.7 %reduce-scatter.8.cloned.1.call-start = ((), (), s32[]{:S(2)}) async-start(), calls=%async_computation.8 | async-start | bytes 4718592 | tf_op jit(solution)/shard_map/reduce_scatter | solution.py:220
  380.5 1.0 copy-start.3
  380.6 1.5 copy-start.24
  380.6 1.5 copy-start.21
  380.6 1.6 copy-start.15
  380.6 12.2 %copy-start.26 = (s32[128]{0:T(128)S(1)}, s32[128]{0:T(128)}, u32[]{:S(2)}) copy-start(s32[128]{0:T(128)} %param.41) | copy-start | bytes 1540
  484.1 15.3 %copy-start.1 = (bf16[4096,160]{0,1:T(8,128)(2,1)S(1)}, bf16[4096,160]{0,1:T(8,128)(2,1)}, u32[]{:S(2)}) copy-start(bf16[4096,160]{0,1:T(8,128)(2,1)} %param.26) | copy-start | bytes 3932164
Sparse Core Ops, SparseCore 0:
  41.5 42.4 all-gather.6
  107.0 43.8 reduce-scatter.5
  153.9 110.0 reduce-scatter.3
  265.5 81.2 all-gather.4
  380.7 52.6 reduce-scatter.7

commit v3 on v2

--- a/solution.py
+++ b/solution.py
@@ -25,20 +25,37 @@
     )
 
 
+def fading_sums(logarithmic_fading_entries):
+    cumulative = jnp.cumsum(logarithmic_fading_entries, axis=1)
+    starts = jnp.concatenate(
+        [jnp.zeros_like(logarithmic_fading_entries[:, :1]), cumulative], axis=1
+    )
+    return cumulative, starts
+
+
+def picked_states(
+    lookup_vectors, payload_vectors, cumulative, starts, starting_memory, approved_guesses
+):
+    draft = lookup_vectors.shape[1]
+    at_accept = jnp.take_along_axis(starts, approved_guesses[:, None, None, None], axis=1)[:, 0]
+    used = jnp.arange(draft)[None, :] < approved_guesses[:, None]
+    coef_exp = jnp.where(used[:, :, None, None], at_accept[:, None] - cumulative, -1e30)
+    weighted = jnp.exp(coef_exp) * lookup_vectors
+    return jnp.exp(at_accept)[..., None] * starting_memory + jnp.einsum(
+        "bshi,bshj->bhij", weighted, payload_vectors, precision=lax.Precision.HIGHEST
+    )
+
+
 def wkv_blocks(
     acceptor_vectors,
     lookup_vectors,
     payload_vectors,
-    logarithmic_fading_entries,
+    cumulative,
+    starts,
     diagonal_boost,
     starting_memory,
-    approved_guesses,
 ):
     draft = acceptor_vectors.shape[1]
-    cumulative = jnp.cumsum(logarithmic_fading_entries, axis=1)
-    starts = jnp.concatenate(
-        [jnp.zeros_like(logarithmic_fading_entries[:, :1]), cumulative], axis=1
-    )
     before = starts[:, :draft]
     from_start = jnp.einsum(
         "bthi,bhij->bthj",
@@ -57,15 +74,7 @@
         jnp.sum(acceptor_vectors * diagonal_boost * lookup_vectors, axis=-1, keepdims=True)
         * payload_vectors
     )
-    outputs = from_start + inner + diagonal_boost_contribution
-    at_accept = jnp.take_along_axis(starts, approved_guesses[:, None, None, None], axis=1)[:, 0]
-    used = jnp.arange(draft)[None, :] < approved_guesses[:, None]
-    coef_exp = jnp.where(used[:, :, None, None], at_accept[:, None] - cumulative, -1e30)
-    weighted = jnp.exp(coef_exp) * lookup_vectors
-    picked = jnp.exp(at_accept)[..., None] * starting_memory + jnp.einsum(
-        "bshi,bshj->bhij", weighted, payload_vectors, precision=lax.Precision.HIGHEST
-    )
-    return (outputs, picked)
+    return from_start + inner + diagonal_boost_contribution
 
 
 def gated_norm(outputs, gate_raw, gain, bias):
@@ -175,21 +184,17 @@
         return lax.psum_scatter(values, "dp", scatter_dimension=0, tiled=True).astype(jnp.float32)
 
     token_rows = row_reqs * draft
-    triple = summed(
-        jnp.concatenate(
-            [
-                partial(3, acceptor_matrix),
-                partial(1, lookup_matrix),
-                partial(2, payload_matrix),
-            ],
-            axis=1,
-        )
-    )
-    acceptor_vectors, lookup_vectors, payload_vectors = jnp.split(triple, 3, axis=1)
-    gate_summed = lax.psum_scatter(
-        partial(4, gating_matrix), "dp", scatter_dimension=0, tiled=True
-    )
-    gate_raw = gate_summed.astype(jnp.float32)
+    pair = jnp.concatenate([partial(1, lookup_matrix), partial(2, payload_matrix)], axis=1)
+    acceptor_matrix, gating_matrix, pair = lax.optimization_barrier(
+        (acceptor_matrix, gating_matrix, pair)
+    )
+    lookup_vectors, payload_vectors = jnp.split(summed(pair), 2, axis=1)
+    late_sum = lax.psum_scatter(
+        jnp.concatenate([partial(3, acceptor_matrix), partial(4, gating_matrix)], axis=1),
+        "dp",
+        scatter_dimension=0,
+        tiled=True,
+    )
     row_narrow = lax.dynamic_index_in_dim(narrow, row_index, 0, keepdims=False)
     decay_inner_rows = row_narrow[:, narrow_width - decay_width :]
     logarithmic_fading_entries = -jnp.exp(
@@ -200,40 +205,12 @@
         return values.reshape(row_reqs, draft, local_heads, GROUP_DIMENSION)
 
     row_accepted = lax.dynamic_slice_in_dim(approved_guesses, row_index * row_reqs, row_reqs)
-    outputs, picked = wkv_blocks(
-        to_heads(acceptor_vectors),
-        to_heads(lookup_vectors),
-        to_heads(payload_vectors),
-        to_heads(logarithmic_fading_entries),
-        diagonal_boost,
-        earlier_memory_matrix,
-        row_accepted,
-    )
-    hidden = gated_norm(
-        outputs.reshape(token_rows, local_heads, GROUP_DIMENSION),
-        gate_raw,
-        groupwise_scaling_factor,
-        groupwise_scaling_offset,
-    )
-    emission_matrix, gate_summed = lax.optimization_barrier((emission_matrix, gate_summed))
-    out_cols = lax.all_gather(emission_matrix, "dp", axis=1, tiled=True)
-    attended = lax.psum_scatter(
-        jnp.dot(hidden, out_cols, preferred_element_type=jnp.float32).astype(jnp.bfloat16),
-        "mp",
-        scatter_dimension=0,
-        tiled=True,
-    ).astype(jnp.float32)
+    lookup_heads, payload_heads = to_heads(lookup_vectors), to_heads(payload_vectors)
+    cumulative, starts = fading_sums(to_heads(logarithmic_fading_entries))
+    picked = picked_states(
+        lookup_heads, payload_heads, cumulative, starts, earlier_memory_matrix, row_accepted
+    )
     own_start = (row_index * group_count + group_index) * own_reqs
-    own_lengths = lax.dynamic_slice_in_dim(usable_guess_amount, own_start, own_reqs)
-    valid_mask = jnp.arange(draft, dtype=jnp.int32)[None, :] < own_lengths[:, None]
-    layer_out = (
-        guess_vectors.astype(jnp.float32)
-        + jnp.where(
-            valid_mask[..., None],
-            attended.reshape(own_reqs, draft, width),
-            jnp.zeros((), jnp.float32),
-        )
-    ).astype(jnp.bfloat16)
     own_accepted = lax.dynamic_slice_in_dim(approved_guesses, own_start, own_reqs)
     edge_rows = jnp.concatenate([preceding_symbol_vector[:, None, :], guess_vectors], axis=1)
     own_chosen = jnp.take_along_axis(edge_rows, own_accepted[:, None, None], axis=1)[:, 0]
@@ -260,7 +237,43 @@
         selected.astype(jnp.int32) * jnp.arange(row_reqs, dtype=jnp.int32)[:, None, None], axis=0
     )
     send_state = picked.astype(jnp.bfloat16)[source_index]
+    send_state, chosen_cols = lax.optimization_barrier((send_state, chosen_cols))
     recv_state = lax.all_to_all(send_state, "dp", split_axis=0, concat_axis=0, tiled=True)
+    late_sum, send_state = lax.optimization_barrier((late_sum, send_state))
+    acceptor_vectors, gate_raw = jnp.split(late_sum.astype(jnp.float32), 2, axis=1)
+    outputs = wkv_blocks(
+        to_heads(acceptor_vectors),
+        lookup_heads,
+        payload_heads,
+        cumulative,
+        starts,
+        diagonal_boost,
+        earlier_memory_matrix,
+    )
+    hidden = gated_norm(
+        outputs.reshape(token_rows, local_heads, GROUP_DIMENSION),
+        gate_raw,
+        groupwise_scaling_factor,
+        groupwise_scaling_offset,
+    )
+    emission_matrix, late_sum = lax.optimization_barrier((emission_matrix, late_sum))
+    out_cols = lax.all_gather(emission_matrix, "dp", axis=1, tiled=True)
+    attended = lax.psum_scatter(
+        jnp.dot(hidden, out_cols, preferred_element_type=jnp.float32).astype(jnp.bfloat16),
+        "mp",
+        scatter_dimension=0,
+        tiled=True,
+    ).astype(jnp.float32)
+    own_lengths = lax.dynamic_slice_in_dim(usable_guess_amount, own_start, own_reqs)
+    valid_mask = jnp.arange(draft, dtype=jnp.int32)[None, :] < own_lengths[:, None]
+    layer_out = (
+        guess_vectors.astype(jnp.float32)
+        + jnp.where(
+            valid_mask[..., None],
+            attended.reshape(own_reqs, draft, width),
+            jnp.zeros((), jnp.float32),
+        )
+    ).astype(jnp.bfloat16)
     wanted = row_index * row_reqs + jnp.arange(row_reqs, dtype=jnp.int32)
     total_reqs = destination_slot.shape[0]
     matches = (destination_slot[None, :] == wanted[:, None]).astype(jnp.int32)

time: 515 us -> 490 us (0.951)
  blocking collectives: 114 us -> 49.3 us
  waiting for transfers between devices: 153 us -> 191 us
  other arithmetic: 48.1 us -> 58.3 us
  local copies, waits for them, and re-layouts: 100 us -> 94.4 us
    reduce_scatter x1, waiting for transfers between devices: 102 us -> 18.2 us  [summed(): lax.psum_scatter(values, 'dp', scatter_dimension=0, tiled=True)]
    all_to_all x1, waiting for transfers between devices: 0.01 us -> 79.9 us  [on_device(): lax.all_to_all(send_state, 'dp', split_axis=0, concat_axis=0, tiled=True)]
    all_gather x1, blocking collectives: 79.8 us -> 15.1 us  [on_device(): lax.all_gather(lax.dynamic_slice_in_dim(row_chosen, group_index * local_w...]
    reduce_scatter x1, waiting for transfers between devices: 7.9 us -> 47.4 us  [on_device(): lax.psum_scatter(jnp.concatenate([partial(3, acceptor_matrix), partial(4,...]
    mul x3 -> x0, local copies, waits for them, and re-layouts: 6.48 us -> none  [the longest x2 3.69 us: gated_norm(): spread * lax.rsqrt(variance + norm_eps)]
    reduce_sum x0 -> x1, other arithmetic: none -> 5.69 us  [wkv_blocks(): jnp.sum(acceptor_vectors * diagonal_boost * lookup_vectors, axis=-1, keep...]
    reshape x4 -> x5, local copies, waits for them, and re-layouts: 8.96 us -> 11.7 us  [to_heads(): return values.reshape(row_reqs, draft, local_heads, GROUP_DIMENSION)]
    unnamed x60 -> x46, local copies, waits for them, and re-layouts: 21.1 us -> 20.1 us
  transfers between devices with their start and end apart: 6 -> 6, of which waited for: 3 -> 5; matrix products, arithmetic and copies ran while one was open for 36% -> 36% of each run, Pallas kernels for 0% -> 0%
where the time goes in v3:
time: 490 us; the launch traced here: 485 us
  waiting for transfers between devices  191 us (39%)
  local copies, waits for them, and re-layouts  94.4 us (19%)
  matrix products  71.5 us (15%)
  other arithmetic  58.3 us (12%)
  blocking collectives  49.3 us (10%)
  between operations  14.6 us (3%)
  starting transfers between devices  5.76 us (1%)
    all_to_all x1, waiting for transfers between devices, on_device(): lax.all_to_all(send_state, 'dp', split_axis=0, concat_axis=0, tiled=True)  79.9 us
    reduce_scatter x1, waiting for transfers between devices, on_device(): lax.psum_scatter(jnp.concatenate([partial(3, acceptor_matrix), partial(4,...  47.4 us
    all_gather x1, waiting for transfers between devices, on_device(): packed = lax.all_gather(packed, 'mp', axis=0, tiled=False)  42.4 us
    dot_general x7, matrix products, dot32(): return jnp.dot(left, right, preferred_element_type=jnp.float32)  40.7 us
    all_to_all x1, blocking collectives, on_device(): lax.all_to_all(packed, 'dp', split_axis=0, concat_axis=0, tiled=True)  24.9 us
    unnamed x46, local copies, waits for them, and re-layouts  20.1 us
    reduce_scatter x1, waiting for transfers between devices, summed(): lax.psum_scatter(values, 'dp', scatter_dimension=0, tiled=True)  18.2 us
    reduce_sum x1, other arithmetic, wkv_blocks(): jnp.sum(acceptor_vectors[:, :, None] * lookup_vectors[:, None, :] * jnp.e...  15.2 us
  transfers between devices with their start and end apart: 6, of which 5 were waited for; matrix products, arithmetic and copies ran while one was open for 36% of the time, Pallas kernels for 0%

profile of v3, /device:TPU:0, one launch (start us, length us, event | category | flops | bytes accessed | tf_op | source)
XLA Modules:
  0.0 484.5 jit_solution(17415819732558861520)
XLA Ops:
  16.5 24.9 %all_to_all.10 = bf16[4,82,1024]{2,1,0:T(8,128)(2,1)} all-to-all(bf16[4,82,1024]{2,1,0:T(8,128)(2,1)S(1)} %copy.141), channel_id=1, replica_groups=mesh['dp'=4,'mp'=8] {'dp'}, dimensions={0} | all-to-all | bytes 1343488 | tf_op jit(solution)/shard_map/all_to_all | solution.py:154
  41.6 42.4 %all-gather.7.cloned.1.call-done = bf16[32,82,1024]{2,1,0:T(8,128)(2,1)} async-done(((bf16[4,82,1024]{2,1,0:T(8,128)(2,1)}), bf16[32,82,1024]{2,1,0:T(8,128)(2,1)}) %all-gather.7.cloned.1.call-update) | async-done | bytes 5373968 | tf_op jit(solution)/shard_map/all_gather | solution.py:155
  84.0 3.3 copy.180
  87.3 2.5 slice.101
  90.9 2.3 reshape_reshape.7
  93.2 4.9 %pad_maximum_fusion = bf16[4,8,4,16,1024]{4,3,2,1,0:T(8,128)(2,1)} fusion(bf16[4,8,4,15,1024]{4,3,2,1,0:T(8,128)(2,1)} %bitcast.142, bf16[4,8,4,1,1024]{4,3,2,1,0:T(2,128)(2,1)S(1)} %copy.144), kind=kLoop, calls=%fused_computation.23 | loop fusion | flops 8388608 | bytes 8388608 | tf_op jit(solution)/shard_map/concatenate | solution.py:13
  98.2 9.6 %convolution_convert_fusion.3 = bf16[2048,512]{0,1:T(8,128)(2,1)} fusion(bf16[1024,512]{1,0:T(8,128)(2,1)} %param.34, bf16[2048,1024]{1,0:T(8,128)(2,1)} %bitcast.143, bf16[2048,1024]{1,0:T(8,128)(2,1)} %bitcast.149, f32[1024]{0:T(1024)S(1)} %bitcast.162, bf16[2048,224]{1,0:T(8,128)(2,1)S(1)} %reshape_reshape.7, bf16[5,32,4096]{2,1,0:T(8,128)(2,1)} %param.27, ...), kind=kOutput, calls=%fused_computation.28 | convolution fusion | flops 2297430016 | bytes 12128264 | tf_op jit(solution)/shard_map/dot_general | solution.py:19
  107.8 9.5 %convolution_convert_fusion.4 = bf16[2048,512]{0,1:T(8,128)(2,1)} fusion(bf16[1024,512]{1,0:T(8,128)(2,1)} %param.33, bf16[2048,1024]{1,0:T(8,128)(2,1)} %bitcast.144, bf16[2048,1024]{1,0:T(8,128)(2,1)} %bitcast.150, f32[1024]{0:T(1024)S(1)} %bitcast.161, bf16[2048,224]{1,0:T(8,128)(2,1)S(1)} %reshape_reshape.7, bf16[5,32,4096]{2,1,0:T(8,128)(2,1)} %param.27, ...), kind=kOutput, calls=%fused_computation.29 | convolution fusion | flops 2297430016 | bytes 12128264 | tf_op jit(solution)/shard_map/dot_general | solution.py:19
  117.3 4.8 pad_maximum_fusion.1
  122.3 9.4 %convolution_convert_fusion.1 = bf16[2048,512]{0,1:T(8,128)(2,1)} fusion(bf16[1024,512]{1,0:T(8,128)(2,1)} %param.35, bf16[2048,1024]{1,0:T(8,128)(2,1)} %bitcast.145, bf16[2048,1024]{1,0:T(8,128)(2,1)} %bitcast.151, f32[1024]{0:T(1024)S(1)} %bitcast.160, bf16[2048,224]{1,0:T(8,128)(2,1)S(1)} %reshape_reshape.7, bf16[5,32,4096]{2,1,0:T(8,128)(2,1)} %param.27, ...), kind=kOutput, calls=%fused_computation.26 | convolution fusion | flops 2297430016 | bytes 12128264 | tf_op jit(solution)/shard_map/dot_general | solution.py:19
  131.8 9.5 %convolution_convert_fusion.2 = bf16[2048,512]{0,1:T(8,128)(2,1)} fusion(bf16[1024,512]{1,0:T(8,128)(2,1)} %param.32, bf16[2048,1024]{1,0:T(8,128)(2,1)} %bitcast.146, bf16[2048,1024]{1,0:T(8,128)(2,1)} %bitcast.152, f32[1024]{0:T(1024)S(1)} %bitcast.159, bf16[2048,224]{1,0:T(8,128)(2,1)S(1)} %reshape_reshape.7, bf16[5,32,4096]{2,1,0:T(8,128)(2,1)} %param.27, ...), kind=kOutput, calls=%fused_computation.27 | convolution fusion | flops 2297430016 | bytes 12128264 | tf_op jit(solution)/shard_map/dot_general | solution.py:19
  141.3 4.8 pad_maximum_fusion.2
  148.8 9.3 %all-gather.1 = bf16[8,4,4096]{2,1,0:T(4,128)(2,1)S(1)} all-gather(bf16[1,4,4096]{2,1,0:T(4,128)(2,1)S(1)} %select_bitcast_fusion), channel_id=1, replica_groups=mesh['dp'=4,'mp'=8] {'mp'}, dimensions={0}, use_global_device_ids=true | all-gather | bytes 294912 | tf_op jit(solution)/shard_map/all_gather | solution.py:217
  158.1 15.1 %all_gather.18 = bf16[128,512]{1,0:T(8,128)(2,1)S(1)} all-gather(bf16[32,512]{1,0:T(8,128)(2,1)S(1)} %constant_dynamic-slice_fusion), channel_id=1, replica_groups=mesh['dp'=4,'mp'=8] {'dp'}, dimensions={0}, use_global_device_ids=true | all-gather | bytes 163840 | tf_op jit(solution)/shard_map/all_gather | solution.py:218
  173.5 1.7 reshape.371
  175.6 1.7 reshape.372
  177.3 1.7 fusion.62
  180.6 2.2 gather_fusion.4
  183.0 18.2 %reduce-scatter.6.cloned.1.call-done = bf16[512,1024]{0,1:T(8,128)(2,1)} async-done(((bf16[2048,1024]{0,1:T(8,128)(2,1)}), bf16[512,1024]{0,1:T(8,128)(2,1)}) %reduce-scatter.6.cloned.1.call-update) | async-done | bytes 1048592 | tf_op jit(solution)/shard_map/reduce_scatter | solution.py:184
  201.1 2.8 fusion.58
  203.9 2.6 copy.145
  206.5 2.8 reshape.374
  212.0 2.0 exponential_multiply_fusion.1
  214.0 11.7 %add_convert_fusion = bf16[32,8,64,64]{3,2,1,0:T(8,128)(2,1)} fusion(f32[32,8,64,64]{3,2,1,0:T(8,128)} %param.23, f32[32,8,64]{2,1,0:T(8,128)S(1)} %get-tuple-element.19, f32[32,16,8,64]{3,2,1,0:T(8,128)S(1)} %exponential_multiply_fusion.1, bf16[32,16,8,64]{3,2,1,0:T(8,128)(2,1)S(1)} %reshape.375), kind=kOutput, calls=%fused_computation.16 | convolution fusion | flops 204472320 | bytes 7929856 | tf_op jit(solution)/shard_map/bshi,bshj->bhij/dot_general | solution.py:44
  225.6 7.8 %gather_fusion = bf16[64,8,64,64]{3,2,1,0:T(8,128)(2,1)} fusion(bf16[32,8,64,64]{3,2,1,0:T(8,128)(2,1)} %add_convert_fusion, s32[1024]{0:T(1024)S(1)} %pad_clamp_fusion.2), kind=kCustom, calls=%fused_computation | custom fusion | bytes 8388864 | tf_op jit(solution)/shard_map/gather | solution.py:239
  233.5 47.4 %reduce-scatter.4.cloned.1.call-done = bf16[512,1024]{0,1:T(8,128)(2,1)} async-done(((bf16[2048,1024]{0,1:T(8,128)(2,1)}), bf16[512,1024]{0,1:T(8,128)(2,1)}) %reduce-scatter.4.cloned.1.call-update) | async-done | bytes 1048592 | tf_op jit(solution)/shard_map/reduce_scatter | solution.py:192
  280.9 2.1 split.21
  283.0 2.8 convert_element_type.106
  285.9 2.6 copy.155
  288.4 2.8 reshape.378
  291.3 2.6 copy.150
  293.9 2.7 reshape.377
  296.6 5.7 %multiply_reduce_fusion.2 = (f32[32,16,8]{2,1,0:T(8,128)}, f32[32,16,8,64]{3,2,1,0:T(8,128)}, f32[32,16,8,64]{3,2,1,0:T(8,128)}) fusion(f32[32,16,8,64]{3,2,1,0:T(8,128)} %reshape.374, f32[32,16,8,64]{3,2,1,0:T(8,128)} %reshape.377, f32[8,64]{1,0:T(8,128)S(1)} %copy-done.12, f32[32,16,8,64]{3,2,1,0:T(8,128)S(1)} %fusion.62), kind=kLoop, calls=%fused_computation.37 | loop fusion | flops 1044480 | bytes 5261312 | tf_op jit(solution)/shard_map/reduce_sum | solution.py:74
  303.3 15.2 %multiply_reduce_fusion = f32[32,16,16,8]{3,2,1,0:T(8,128)} fusion(f32[32,16,8,64]{3,2,1,0:T(8,128)S(1)} %fusion.62, f32[32,16,8,64]{3,2,1,0:T(8,128)} %get-tuple-element.25, f32[32,16,8,64]{3,2,1,0:T(8,128)} %reshape.374, f32[32,16,8,64]{3,2,1,0:T(8,128)} %reshape.377, pred[16,16]{1,0:T(8,128)(4,1)S(1)} %iota_compare_fusion.2), kind=kLoop, calls=%fused_computation.6 | loop fusion | flops 20905984 | bytes 4456704 | tf_op jit(solution)/shard_map/reduce_sum | solution.py:69
  318.5 4.4 copy.153
  323.0 9.8 %fusion.8 = f32[32,8,16,64]{3,2,1,0:T(8,128)S(1)} fusion(f32[32,8,64,64]{3,2,1,0:T(8,128)} %param.23, f32[32,16,8,64]{3,2,1,0:T(8,128)S(1)} %copy-done.6), kind=kOutput, calls=%fused_computation.33 | convolution fusion | flops 201326592 | bytes 6291456 | tf_op jit(solution)/shard_map/bthi,bhij->bthj/dot_general | solution.py:60
  332.8 2.6 fusion.60
  336.4 9.5 %reshape.442 = bf16[4,2,262144]{2,1,0:T(2,128)(2,1)} reshape(bf16[4,16,8,64,64]{4,3,2,1,0:T(8,128)(2,1)} %bitcast.135) | data formatting | bytes 8388608
  346.0 2.2 copy.157
  348.2 1.9 reshape.379
  354.2 5.2 %all-to-all-start.1 = ((bf16[4,2,262144]{2,1,0:T(2,128)(2,1)}), bf16[4,2,262144]{2,1,0:T(2,128)(2,1)}, u32[]{:S(2)}, u32[]{:S(2)}) async-start(bf16[4,2,262144]{2,1,0:T(2,128)(2,1)} %reshape.442), calls=%async_computation.4 | async-start | bytes 8388608 | tf_op jit(solution)/shard_map/all_to_all | solution.py:241
  360.9 2.8 all-gather.5.cloned.1.call-done
  363.7 6.7 %convolution_convert_fusion = bf16[512,4096]{1,0:T(8,128)(2,1)} fusion(bf16[512,512]{0,1:T(8,128)(2,1)} %fusion.22, bf16[512,4096]{1,0:T(8,128)(2,1)} %all-gather.5.cloned.1.call-done), kind=kOutput, calls=%fused_computation.17 | convolution fusion | flops 2149580800 | bytes 8912896 | tf_op jit(solution)/shard_map/dot_general | solution.py:262
  373.4 79.9 %all-to-all-done.1 = bf16[4,2,262144]{2,1,0:T(2,128)(2,1)} async-done(((bf16[4,2,262144]{2,1,0:T(2,128)(2,1)}), bf16[4,2,262144]{2,1,0:T(2,128)(2,1)}, u32[]{:S(2)}, u32[]{:S(2)}) %all-to-all-start.1) | async-done | bytes 4194336 | tf_op jit(solution)/shard_map/all_to_all | solution.py:241
  453.2 9.3 %reshape.443 = bf16[4,16,8,64,64]{4,3,2,1,0:T(8,128)(2,1)} reshape(bf16[4,2,262144]{2,1,0:T(2,128)(2,1)} %all-to-all-done.1) | data formatting | bytes 8388608
  462.5 6.5 %gather_fusion.2 = bf16[32,8,64,64]{3,2,1,0:T(8,128)(2,1)} fusion(bf16[64,8,64,64]{3,2,1,0:T(8,128)(2,1)} %bitcast.141, s32[1024]{0:T(1024)S(1)} %pad_clamp_fusion), kind=kCustom, calls=%fused_computation.2 | custom fusion | bytes 4194432 | tf_op jit(solution)/shard_map/gather | solution.py:282
  469.0 6.7 %convert_element_type.110 = f32[32,8,64,64]{3,2,1,0:T(8,128)} convert(bf16[32,8,64,64]{3,2,1,0:T(8,128)(2,1)} %gather_fusion.2) | non-fusion elementwise | flops 1048576 | bytes 6291456 | tf_op jit(solution)/shard_map/convert_element_type | solution.py:284
  475.7 2.1 fusion.18
  (130 shorter events, 28.8 us)
Async XLA Ops:
  7.2 6.1 %copy-start = (bf16[4096,160]{0,1:T(8,128)(2,1)S(1)}, bf16[4096,160]{0,1:T(8,128)(2,1)}, u32[]{:S(2)}) copy-start(bf16[4096,160]{0,1:T(8,128)(2,1)} %param.26) | copy-start | bytes 3932164
  7.2 6.6 %slice-start.1 = ((f32[5,4096]{1,0:T(8,128)}), f32[1,4096]{1,0:T(1,128)S(1)}, s32[]{:S(2)}) async-start(f32[5,4096]{1,0:T(8,128)} %param.25), calls=%async_computation.11 | async-start | bytes 32768 | tf_op jit(solution)/shard_map/slice | solution.py:131
  7.2 6.6 %copy-start.2 = (bf16[4,16,4096]{2,1,0:T(8,128)(2,1)S(1)}, bf16[4,16,4096]{2,1,0:T(8,128)(2,1)}, u32[]{:S(2)}) copy-start(bf16[4,16,4096]{2,1,0:T(8,128)(2,1)} %param.21) | copy-start | bytes 1572868
  7.2 76.8 %all-gather.7.cloned.1.call-start = ((), (), s32[]{:S(2)}) async-start(), calls=%async_computation.9 | async-start | bytes 6488064 | tf_op jit(solution)/shard_map/all_gather | solution.py:155
  13.8 27.7 %copy-start.10 = (f32[5,4096]{1,0:T(8,128)S(1)}, f32[5,4096]{1,0:T(8,128)}, u32[]{:S(2)}) copy-start(f32[5,4096]{1,0:T(8,128)} %param.25) | copy-start | bytes 245764
  41.4 159.7 %reduce-scatter.6.cloned.1.call-start = ((), (), s32[]{:S(2)}) async-start(), calls=%async_computation.6 | async-start | bytes 5242880 | tf_op jit(solution)/shard_map/reduce_scatter | solution.py:184
  122.1 158.8 %reduce-scatter.4.cloned.1.call-start = ((), (), s32[]{:S(2)}) async-start(), calls=%async_computation.5 | async-start | bytes 5242880 | tf_op jit(solution)/shard_map/reduce_scatter | solution.py:192
  146.1 0.7 copy-start.18
  146.1 1.4 copy-start.14
  146.1 1.5 copy-start.9
  146.1 29.1 %copy-start.11 = (bf16[64,512]{1,0:T(8,128)(2,1)S(1)}, bf16[64,512]{1,0:T(8,128)(2,1)}, u32[]{:S(2)}) copy-start(bf16[64,512]{1,0:T(8,128)(2,1)} %param.30) | copy-start | bytes 196612
  146.1 29.1 %copy-start.13 = (f32[512]{0:T(512)S(1)}, f32[512]{0:T(512)}, u32[]{:S(2)}) copy-start(f32[512]{0:T(512)} %param.28) | copy-start | bytes 6148
  146.1 217.6 %all-gather.5.cloned.1.call-start = ((), (), s32[]{:S(2)}) async-start(), calls=%async_computation.7 | async-start | bytes 5242880 | tf_op jit(solution)/shard_map/all_gather | solution.py:260
  203.9 5.3 %slice-start = ((bf16[512,1024]{0,1:T(8,128)(2,1)}), bf16[512,512]{0,1:T(8,128)(2,1)S(1)}, s32[]{:S(2)}) async-start(bf16[512,1024]{0,1:T(8,128)(2,1)} %reduce-scatter.6.cloned.1.call-done), calls=%async_computation.10 | async-start | bytes 1048576 | tf_op jit(solution)/shard_map/split | solution.py:191
  288.4 8.1 %copy-start.12 = (f32[8,64]{1,0:T(8,128)S(1)}, f32[8,64]{1,0:T(8,128)}, u32[]{:S(2)}) copy-start(f32[8,64]{1,0:T(8,128)} %param.31) | copy-start | bytes 6148
  318.5 4.4 copy-start.6
  323.0 9.8 %copy-start.4 = (f32[32,16,16,8]{2,1,3,0:T(8,128)S(1)}, f32[32,16,16,8]{2,1,3,0:T(8,128)}, u32[]{:S(2)}) copy-start(f32[32,16,16,8]{2,1,3,0:T(8,128)} %copy.153) | copy-start | bytes 786436
  323.0 9.8 %copy-start.5 = (f32[32,16,8,64]{3,2,1,0:T(8,128)S(1)}, f32[32,16,8,64]{3,2,1,0:T(8,128)}, u32[]{:S(2)}) copy-start(f32[32,16,8,64]{3,2,1,0:T(8,128)} %reshape.378) | copy-start | bytes 3145732
  354.1 5.5 %copy-start.7 = (f32[512,1024]{0,1:T(8,128)S(1)}, f32[512,1024]{0,1:T(8,128)}, u32[]{:S(2)}) copy-start(f32[512,1024]{0,1:T(8,128)} %convert_element_type.106) | copy-start | bytes 6291460
  354.1 5.5 %copy-start.8 = (f32[512,512]{0,1:T(8,128)S(1)}, f32[512,512]{0,1:T(8,128)}, u32[]{:S(2)}) copy-start(f32[512,512]{0,1:T(8,128)} %copy.160) | copy-start | bytes 3145732
  354.2 5.5 %copy-start.15 = (f32[512]{0:T(512)S(1)}, f32[512]{0:T(512)}, u32[]{:S(2)}) copy-start(f32[512]{0:T(512)} %param.38) | copy-start | bytes 6148
  354.2 5.5 %copy-start.16 = (f32[512]{0:T(512)S(1)}, f32[512]{0:T(512)}, u32[]{:S(2)}) copy-start(f32[512]{0:T(512)} %param.37) | copy-start | bytes 6148
  354.2 99.0 %all-to-all-start.1 = ((bf16[4,2,262144]{2,1,0:T(2,128)(2,1)}), bf16[4,2,262144]{2,1,0:T(2,128)(2,1)}, u32[]{:S(2)}, u32[]{:S(2)}) async-start(bf16[4,2,262144]{2,1,0:T(2,128)(2,1)} %reshape.442), calls=%async_computation.4 | async-start | bytes 8388608 | tf_op jit(solution)/shard_map/all_to_all | solution.py:241
  359.4 116.3 %reduce-scatter.8.cloned.1.call-start = ((), (), s32[]{:S(2)}) async-start(), calls=%async_computation.8 | async-start | bytes 4718592 | tf_op jit(solution)/shard_map/reduce_scatter | solution.py:261
  370.4 0.7 copy-start.17
  370.4 0.7 copy-start.19
  462.5 15.3 %copy-start.1 = (bf16[4096,160]{0,1:T(8,128)(2,1)S(1)}, bf16[4096,160]{0,1:T(8,128)(2,1)}, u32[]{:S(2)}) copy-start(bf16[4096,160]{0,1:T(8,128)(2,1)} %param.26) | copy-start | bytes 3932164
  469.0 6.7 %copy-start.3 = (bf16[4,16,4096]{2,1,0:T(8,128)(2,1)S(1)}, bf16[4,16,4096]{2,1,0:T(8,128)(2,1)}, u32[]{:S(2)}) copy-start(bf16[4,16,4096]{2,1,0:T(8,128)(2,1)} %param.21) | copy-start | bytes 1572868
Sparse Core Ops, SparseCore 0:
  41.5 42.4 all-gather.6
  122.2 78.8 reduce-scatter.5
  203.5 77.2 reduce-scatter.3
  282.3 81.3 all-gather.4
  370.5 49.8 reduce-scatter.7

commit v4 on v3

--- a/solution.py
+++ b/solution.py
@@ -236,7 +236,9 @@
     source_index = jnp.sum(
         selected.astype(jnp.int32) * jnp.arange(row_reqs, dtype=jnp.int32)[:, None, None], axis=0
     )
-    send_state = picked.astype(jnp.bfloat16)[source_index]
+    send_state = picked.astype(jnp.bfloat16)[source_index].reshape(
+        row_groups, capacity, local_heads * GROUP_DIMENSION * GROUP_DIMENSION // 128, 128
+    )
     send_state, chosen_cols = lax.optimization_barrier((send_state, chosen_cols))
     recv_state = lax.all_to_all(send_state, "dp", split_axis=0, concat_axis=0, tiled=True)
     late_sum, send_state = lax.optimization_barrier((late_sum, send_state))
@@ -279,9 +281,11 @@
     matches = (destination_slot[None, :] == wanted[:, None]).astype(jnp.int32)
     which = jnp.sum(matches * jnp.arange(total_reqs, dtype=jnp.int32)[None, :], axis=1)
     flat_index = which // row_reqs * capacity + ranks.reshape(-1)[which]
-    next_state = recv_state.reshape(
-        row_groups * capacity, local_heads, GROUP_DIMENSION, GROUP_DIMENSION
-    )[flat_index].astype(jnp.float32)
+    next_state = (
+        recv_state.reshape(row_groups * capacity, -1, 128)[flat_index]
+        .reshape(row_reqs, local_heads, GROUP_DIMENSION, GROUP_DIMENSION)
+        .astype(jnp.float32)
+    )
     next_edge = chosen_cols[which]
     return (layer_out, next_state, next_edge)
 

time: 490 us -> 478 us (0.976)
  other arithmetic: 58.3 us -> 52.9 us
    all_gather x1, waiting for transfers between devices: 2.82 us -> 43.9 us  [on_device(): out_cols = lax.all_gather(emission_matrix, 'dp', axis=1, tiled=True)]
    all_to_all x1, waiting for transfers between devices: 79.9 us -> 48.1 us  [on_device(): lax.all_to_all(send_state, 'dp', split_axis=0, concat_axis=0, tiled=True)]
    unnamed x46 -> x40, local copies, waits for them, and re-layouts: 20.1 us -> 1.23 us
    reshape x0 -> x1, local copies, waits for them, and re-layouts: none -> 11.3 us  [on_device(): picked.astype(jnp.bfloat16)[source_index]]
    reduce_scatter x1, waiting for transfers between devices: 47.4 us -> 36.1 us  [on_device(): lax.psum_scatter(jnp.concatenate([partial(3, acceptor_matrix), partial(4,...]
    convert_element_type x1 -> x0, other arithmetic: 6.72 us -> none  [on_device(): next_state = recv_state.reshape(row_groups * capacity, local_heads, GROUP...]
    convert_element_type x0 -> x1, local copies, waits for them, and re-layouts: none -> 6.63 us  [on_device(): next_state = recv_state.reshape(row_groups * capacity, -1, 128)[flat_inde...]
  transfers between devices with their start and end apart: 6 -> 6, of which waited for: 5 -> 5; matrix products, arithmetic and copies ran while one was open for 36% -> 35% of each run, Pallas kernels for 0% -> 0%
where the time goes in v4:
time: 478 us; the launch traced here: 473 us
  waiting for transfers between devices  189 us (40%)
  local copies, waits for them, and re-layouts  91 us (19%)
  matrix products  71.3 us (15%)
  other arithmetic  52.9 us (11%)
  blocking collectives  49.3 us (10%)
  between operations  14.5 us (3%)
  starting transfers between devices  5.31 us (1%)
    all_to_all x1, waiting for transfers between devices, on_device(): lax.all_to_all(send_state, 'dp', split_axis=0, concat_axis=0, tiled=True)  48.1 us
    all_gather x1, waiting for transfers between devices, on_device(): out_cols = lax.all_gather(emission_matrix, 'dp', axis=1, tiled=True)  43.9 us
    all_gather x1, waiting for transfers between devices, on_device(): packed = lax.all_gather(packed, 'mp', axis=0, tiled=False)  42.4 us
    dot_general x7, matrix products, dot32(): return jnp.dot(left, right, preferred_element_type=jnp.float32)  40.7 us
    reduce_scatter x1, waiting for transfers between devices, on_device(): lax.psum_scatter(jnp.concatenate([partial(3, acceptor_matrix), partial(4,...  36.1 us
    all_to_all x1, blocking collectives, on_device(): lax.all_to_all(packed, 'dp', split_axis=0, concat_axis=0, tiled=True)  24.9 us
    reduce_scatter x1, waiting for transfers between devices, summed(): lax.psum_scatter(values, 'dp', scatter_dimension=0, tiled=True)  18.2 us
    reduce_sum x1, other arithmetic, wkv_blocks(): jnp.sum(acceptor_vectors[:, :, None] * lookup_vectors[:, None, :] * jnp.e...  15.6 us
  transfers between devices with their start and end apart: 6, of which 5 were waited for; matrix products, arithmetic and copies ran while one was open for 35% of the time, Pallas kernels for 0%

profile of v4, /device:TPU:0, one launch (start us, length us, event | category | flops | bytes accessed | tf_op | source)
XLA Modules:
  0.0 473.0 jit_solution(15042639837018675619)
XLA Ops:
  16.5 24.9 %all_to_all.10 = bf16[4,82,1024]{2,1,0:T(8,128)(2,1)} all-to-all(bf16[4,82,1024]{2,1,0:T(8,128)(2,1)S(1)} %copy.141), channel_id=1, replica_groups=mesh['dp'=4,'mp'=8] {'dp'}, dimensions={0} | all-to-all | bytes 1343488 | tf_op jit(solution)/shard_map/all_to_all | solution.py:154
  41.6 42.4 %all-gather.7.cloned.1.call-done = bf16[32,82,1024]{2,1,0:T(8,128)(2,1)} async-done(((bf16[4,82,1024]{2,1,0:T(8,128)(2,1)}), bf16[32,82,1024]{2,1,0:T(8,128)(2,1)}) %all-gather.7.cloned.1.call-update) | async-done | bytes 5373968 | tf_op jit(solution)/shard_map/all_gather | solution.py:155
  84.0 3.3 copy.180
  87.3 2.5 slice.101
  90.9 2.3 reshape_reshape.7
  93.2 5.0 %pad_maximum_fusion = bf16[4,8,4,16,1024]{4,3,2,1,0:T(8,128)(2,1)} fusion(bf16[4,8,4,15,1024]{4,3,2,1,0:T(8,128)(2,1)} %bitcast.141, bf16[4,8,4,1,1024]{4,3,2,1,0:T(2,128)(2,1)S(1)} %copy.144), kind=kLoop, calls=%fused_computation.23 | loop fusion | flops 8388608 | bytes 8388608 | tf_op jit(solution)/shard_map/concatenate | solution.py:13
  98.2 9.6 %convolution_convert_fusion.3 = bf16[2048,512]{0,1:T(8,128)(2,1)} fusion(bf16[1024,512]{1,0:T(8,128)(2,1)} %param.34, bf16[2048,1024]{1,0:T(8,128)(2,1)} %bitcast.142, bf16[2048,1024]{1,0:T(8,128)(2,1)} %bitcast.148, f32[1024]{0:T(1024)S(1)} %bitcast.161, bf16[2048,224]{1,0:T(8,128)(2,1)S(1)} %reshape_reshape.7, bf16[5,32,4096]{2,1,0:T(8,128)(2,1)} %param.27, ...), kind=kOutput, calls=%fused_computation.28 | convolution fusion | flops 2297430016 | bytes 12128264 | tf_op jit(solution)/shard_map/dot_general | solution.py:19
  107.8 9.5 %convolution_convert_fusion.4 = bf16[2048,512]{0,1:T(8,128)(2,1)} fusion(bf16[1024,512]{1,0:T(8,128)(2,1)} %param.33, bf16[2048,1024]{1,0:T(8,128)(2,1)} %bitcast.143, bf16[2048,1024]{1,0:T(8,128)(2,1)} %bitcast.149, f32[1024]{0:T(1024)S(1)} %bitcast.160, bf16[2048,224]{1,0:T(8,128)(2,1)S(1)} %reshape_reshape.7, bf16[5,32,4096]{2,1,0:T(8,128)(2,1)} %param.27, ...), kind=kOutput, calls=%fused_computation.29 | convolution fusion | flops 2297430016 | bytes 12128264 | tf_op jit(solution)/shard_map/dot_general | solution.py:19
  117.3 4.8 %pad_maximum_fusion.1 = bf16[2048,1024]{0,1:T(8,128)(2,1)} fusion(bf16[2048,512]{0,1:T(8,128)(2,1)} %convolution_convert_fusion.3, bf16[2048,512]{0,1:T(8,128)(2,1)} %convolution_convert_fusion.4), kind=kLoop, calls=%fused_computation.24 | loop fusion | flops 8388608 | bytes 8388608 | tf_op jit(solution)/shard_map/concatenate | solution.py:187
  122.4 9.4 %convolution_convert_fusion.1 = bf16[2048,512]{0,1:T(8,128)(2,1)} fusion(bf16[1024,512]{1,0:T(8,128)(2,1)} %param.35, bf16[2048,1024]{1,0:T(8,128)(2,1)} %bitcast.144, bf16[2048,1024]{1,0:T(8,128)(2,1)} %bitcast.150, f32[1024]{0:T(1024)S(1)} %bitcast.159, bf16[2048,224]{1,0:T(8,128)(2,1)S(1)} %reshape_reshape.7, bf16[5,32,4096]{2,1,0:T(8,128)(2,1)} %param.27, ...), kind=kOutput, calls=%fused_computation.26 | convolution fusion | flops 2297430016 | bytes 12128264 | tf_op jit(solution)/shard_map/dot_general | solution.py:19
  131.8 9.5 %convolution_convert_fusion.2 = bf16[2048,512]{0,1:T(8,128)(2,1)} fusion(bf16[1024,512]{1,0:T(8,128)(2,1)} %param.32, bf16[2048,1024]{1,0:T(8,128)(2,1)} %bitcast.145, bf16[2048,1024]{1,0:T(8,128)(2,1)} %bitcast.151, f32[1024]{0:T(1024)S(1)} %bitcast.158, bf16[2048,224]{1,0:T(8,128)(2,1)S(1)} %reshape_reshape.7, bf16[5,32,4096]{2,1,0:T(8,128)(2,1)} %param.27, ...), kind=kOutput, calls=%fused_computation.27 | convolution fusion | flops 2297430016 | bytes 12128264 | tf_op jit(solution)/shard_map/dot_general | solution.py:19
  141.3 4.8 %pad_maximum_fusion.2 = bf16[2048,1024]{0,1:T(8,128)(2,1)} fusion(bf16[2048,512]{0,1:T(8,128)(2,1)} %convolution_convert_fusion.1, bf16[2048,512]{0,1:T(8,128)(2,1)} %convolution_convert_fusion.2), kind=kLoop, calls=%fused_computation.25 | loop fusion | flops 8388608 | bytes 8388608 | tf_op jit(solution)/shard_map/concatenate | solution.py:193
  148.8 9.3 %all-gather.1 = bf16[8,4,4096]{2,1,0:T(4,128)(2,1)S(1)} all-gather(bf16[1,4,4096]{2,1,0:T(4,128)(2,1)S(1)} %select_bitcast_fusion), channel_id=1, replica_groups=mesh['dp'=4,'mp'=8] {'mp'}, dimensions={0}, use_global_device_ids=true | all-gather | bytes 294912 | tf_op jit(solution)/shard_map/all_gather | solution.py:217
  158.2 15.1 %all_gather.18 = bf16[128,512]{1,0:T(8,128)(2,1)S(1)} all-gather(bf16[32,512]{1,0:T(8,128)(2,1)S(1)} %constant_dynamic-slice_fusion), channel_id=1, replica_groups=mesh['dp'=4,'mp'=8] {'dp'}, dimensions={0}, use_global_device_ids=true | all-gather | bytes 163840 | tf_op jit(solution)/shard_map/all_gather | solution.py:218
  173.5 1.7 reshape.377
  175.6 1.7 reshape.378
  177.4 1.7 fusion.62
  180.6 2.2 gather_fusion.4
  183.0 18.2 %reduce-scatter.6.cloned.1.call-done = bf16[512,1024]{0,1:T(8,128)(2,1)} async-done(((bf16[2048,1024]{0,1:T(8,128)(2,1)}), bf16[512,1024]{0,1:T(8,128)(2,1)}) %reduce-scatter.6.cloned.1.call-update) | async-done | bytes 1048592 | tf_op jit(solution)/shard_map/reduce_scatter | solution.py:184
  201.2 2.8 fusion.58
  204.0 2.6 copy.145
  206.5 2.8 reshape.380
  212.0 2.0 exponential_multiply_fusion.1
  214.0 11.7 %add_convert_fusion = bf16[32,8,64,64]{3,2,1,0:T(8,128)(2,1)} fusion(f32[32,8,64,64]{3,2,1,0:T(8,128)} %param.23, f32[32,8,64]{2,1,0:T(8,128)S(1)} %get-tuple-element.19, f32[32,16,8,64]{3,2,1,0:T(8,128)S(1)} %exponential_multiply_fusion.1, bf16[32,16,8,64]{3,2,1,0:T(8,128)(2,1)S(1)} %reshape.381), kind=kOutput, calls=%fused_computation.16 | convolution fusion | flops 204472320 | bytes 7929856 | tf_op jit(solution)/shard_map/bshi,bshj->bhij/dot_general | solution.py:44
  225.7 7.8 %gather_fusion = bf16[64,8,64,64]{3,2,1,0:T(8,128)(2,1)} fusion(bf16[32,8,64,64]{3,2,1,0:T(8,128)(2,1)} %add_convert_fusion, s32[1024]{0:T(1024)S(1)} %pad_clamp_fusion.2), kind=kCustom, calls=%fused_computation | custom fusion | bytes 8388864 | tf_op jit(solution)/shard_map/gather | solution.py:239
  233.5 11.3 %reshape.383 = bf16[4,16,256,128]{3,2,1,0:T(8,128)(2,1)} reshape(bf16[64,8,64,64]{3,2,1,0:T(8,128)(2,1)} %gather_fusion) | data formatting | bytes 8388608 | tf_op jit(solution)/shard_map/reshape | solution.py:239
  244.8 36.1 %reduce-scatter.4.cloned.1.call-done = bf16[512,1024]{0,1:T(8,128)(2,1)} async-done(((bf16[2048,1024]{0,1:T(8,128)(2,1)}), bf16[512,1024]{0,1:T(8,128)(2,1)}) %reduce-scatter.4.cloned.1.call-update) | async-done | bytes 1048592 | tf_op jit(solution)/shard_map/reduce_scatter | solution.py:192
  280.9 2.2 split.21
  283.1 2.8 convert_element_type.109
  285.9 2.5 copy.155
  288.4 2.8 reshape.385
  291.2 2.5 copy.150
  293.8 2.7 reshape.384
  296.5 5.7 %multiply_reduce_fusion.2 = (f32[32,16,8]{2,1,0:T(8,128)}, f32[32,16,8,64]{3,2,1,0:T(8,128)}, f32[32,16,8,64]{3,2,1,0:T(8,128)}) fusion(f32[32,16,8,64]{3,2,1,0:T(8,128)} %reshape.380, f32[32,16,8,64]{3,2,1,0:T(8,128)} %reshape.384, f32[8,64]{1,0:T(8,128)S(1)} %copy-done.10, f32[32,16,8,64]{3,2,1,0:T(8,128)S(1)} %fusion.62), kind=kLoop, calls=%fused_computation.37 | loop fusion | flops 1044480 | bytes 5261312 | tf_op jit(solution)/shard_map/reduce_sum | solution.py:74
  303.3 15.6 %multiply_reduce_fusion = f32[32,16,16,8]{3,2,1,0:T(8,128)} fusion(f32[32,16,8,64]{3,2,1,0:T(8,128)S(1)} %fusion.62, f32[32,16,8,64]{3,2,1,0:T(8,128)} %get-tuple-element.25, f32[32,16,8,64]{3,2,1,0:T(8,128)} %reshape.380, f32[32,16,8,64]{3,2,1,0:T(8,128)} %reshape.384, pred[16,16]{1,0:T(8,128)(4,1)S(1)} %iota_compare_fusion.2), kind=kLoop, calls=%fused_computation.6 | loop fusion | flops 20905984 | bytes 4456704 | tf_op jit(solution)/shard_map/reduce_sum | solution.py:69
  318.9 4.0 copy.153
  322.9 9.8 %fusion.8 = f32[32,8,16,64]{3,2,1,0:T(8,128)S(1)} fusion(f32[32,8,64,64]{3,2,1,0:T(8,128)} %param.23, f32[32,16,8,64]{3,2,1,0:T(8,128)S(1)} %copy-done.6), kind=kOutput, calls=%fused_computation.33 | convolution fusion | flops 201326592 | bytes 6291456 | tf_op jit(solution)/shard_map/bthi,bhij->bthj/dot_general | solution.py:60
  332.7 2.6 fusion.60
  336.4 4.9 %all-to-all-start.1 = ((bf16[4,16,256,128]{3,2,1,0:T(8,128)(2,1)}), bf16[4,16,256,128]{3,2,1,0:T(8,128)(2,1)}, u32[]{:S(2)}, u32[]{:S(2)}) async-start(bf16[4,16,256,128]{3,2,1,0:T(8,128)(2,1)} %reshape.383), calls=%async_computation.4 | async-start | bytes 8388608 | tf_op jit(solution)/shard_map/all_to_all | solution.py:243
  341.4 2.2 copy.157
  343.6 2.1 reshape.386
  349.7 2.0 fusion.22
  351.7 43.9 %all-gather.5.cloned.1.call-done = bf16[512,4096]{1,0:T(8,128)(2,1)} async-done(((bf16[512,1024]{1,0:T(8,128)(2,1)}), bf16[512,4096]{1,0:T(8,128)(2,1)}) %all-gather.5.cloned.1.call-update) | async-done | bytes 4194320 | tf_op jit(solution)/shard_map/all_gather | solution.py:262
  395.6 6.5 %convolution_convert_fusion = bf16[512,4096]{1,0:T(8,128)(2,1)} fusion(bf16[512,512]{0,1:T(8,128)(2,1)S(1)} %fusion.22, bf16[512,4096]{1,0:T(8,128)(2,1)} %all-gather.5.cloned.1.call-done), kind=kOutput, calls=%fused_computation.17 | convolution fusion | flops 2149580800 | bytes 8912896 | tf_op jit(solution)/shard_map/dot_general | solution.py:264
  405.1 48.1 %all-to-all-done.1 = bf16[4,16,256,128]{3,2,1,0:T(8,128)(2,1)} async-done(((bf16[4,16,256,128]{3,2,1,0:T(8,128)(2,1)}), bf16[4,16,256,128]{3,2,1,0:T(8,128)(2,1)}, u32[]{:S(2)}, u32[]{:S(2)}) %all-to-all-start.1) | async-done | bytes 4194336 | tf_op jit(solution)/shard_map/all_to_all | solution.py:243
  453.2 4.4 gather_fusion.2
  457.6 6.6 %reshape.395 = f32[32,8,64,64]{3,2,1,0:T(8,128)} reshape(bf16[32,256,128]{2,1,0:T(8,128)(2,1)} %gather_fusion.2) | data formatting | bytes 6291456 | tf_op jit(solution)/shard_map/convert_element_type | solution.py:287
  464.2 2.1 fusion.18
  (125 shorter events, 27.4 us)
Async XLA Ops:
  7.2 6.1 %copy-start = (bf16[4096,160]{0,1:T(8,128)(2,1)S(1)}, bf16[4096,160]{0,1:T(8,128)(2,1)}, u32[]{:S(2)}) copy-start(bf16[4096,160]{0,1:T(8,128)(2,1)} %param.26) | copy-start | bytes 3932164
  7.2 6.6 %slice-start.1 = ((f32[5,4096]{1,0:T(8,128)}), f32[1,4096]{1,0:T(1,128)S(1)}, s32[]{:S(2)}) async-start(f32[5,4096]{1,0:T(8,128)} %param.25), calls=%async_computation.11 | async-start | bytes 32768 | tf_op jit(solution)/shard_map/slice | solution.py:131
  7.2 6.6 %copy-start.2 = (bf16[4,16,4096]{2,1,0:T(8,128)(2,1)S(1)}, bf16[4,16,4096]{2,1,0:T(8,128)(2,1)}, u32[]{:S(2)}) copy-start(bf16[4,16,4096]{2,1,0:T(8,128)(2,1)} %param.21) | copy-start | bytes 1572868
  7.2 76.8 %all-gather.7.cloned.1.call-start = ((), (), s32[]{:S(2)}) async-start(), calls=%async_computation.9 | async-start | bytes 6488064 | tf_op jit(solution)/shard_map/all_gather | solution.py:155
  13.8 27.7 %copy-start.8 = (f32[5,4096]{1,0:T(8,128)S(1)}, f32[5,4096]{1,0:T(8,128)}, u32[]{:S(2)}) copy-start(f32[5,4096]{1,0:T(8,128)} %param.25) | copy-start | bytes 245764
  41.4 159.7 %reduce-scatter.6.cloned.1.call-start = ((), (), s32[]{:S(2)}) async-start(), calls=%async_computation.6 | async-start | bytes 5242880 | tf_op jit(solution)/shard_map/reduce_scatter | solution.py:184
  122.1 158.8 %reduce-scatter.4.cloned.1.call-start = ((), (), s32[]{:S(2)}) async-start(), calls=%async_computation.5 | async-start | bytes 5242880 | tf_op jit(solution)/shard_map/reduce_scatter | solution.py:192
  146.1 0.7 copy-start.16
  146.1 1.4 copy-start.12
  146.1 1.5 copy-start.7
  146.1 29.1 %copy-start.9 = (bf16[64,512]{1,0:T(8,128)(2,1)S(1)}, bf16[64,512]{1,0:T(8,128)(2,1)}, u32[]{:S(2)}) copy-start(bf16[64,512]{1,0:T(8,128)(2,1)} %param.30) | copy-start | bytes 196612
  146.1 29.1 %copy-start.11 = (f32[512]{0:T(512)S(1)}, f32[512]{0:T(512)}, u32[]{:S(2)}) copy-start(f32[512]{0:T(512)} %param.28) | copy-start | bytes 6148
  146.2 249.4 %all-gather.5.cloned.1.call-start = ((), (), s32[]{:S(2)}) async-start(), calls=%async_computation.7 | async-start | bytes 5242880 | tf_op jit(solution)/shard_map/all_gather | solution.py:262
  204.0 5.4 %slice-start = ((bf16[512,1024]{0,1:T(8,128)(2,1)}), bf16[512,512]{0,1:T(8,128)(2,1)S(1)}, s32[]{:S(2)}) async-start(bf16[512,1024]{0,1:T(8,128)(2,1)} %reduce-scatter.6.cloned.1.call-done), calls=%async_computation.10 | async-start | bytes 1048576 | tf_op jit(solution)/shard_map/split | solution.py:191
  288.4 8.1 %copy-start.10 = (f32[8,64]{1,0:T(8,128)S(1)}, f32[8,64]{1,0:T(8,128)}, u32[]{:S(2)}) copy-start(f32[8,64]{1,0:T(8,128)} %param.31) | copy-start | bytes 6148
  318.9 4.0 copy-start.6
  322.9 9.8 %copy-start.4 = (f32[32,16,16,8]{2,1,3,0:T(8,128)S(1)}, f32[32,16,16,8]{2,1,3,0:T(8,128)}, u32[]{:S(2)}) copy-start(f32[32,16,16,8]{2,1,3,0:T(8,128)} %copy.153) | copy-start | bytes 786436
  322.9 9.8 %copy-start.5 = (f32[32,16,8,64]{3,2,1,0:T(8,128)S(1)}, f32[32,16,8,64]{3,2,1,0:T(8,128)}, u32[]{:S(2)}) copy-start(f32[32,16,8,64]{3,2,1,0:T(8,128)} %reshape.385) | copy-start | bytes 3145732
  336.4 116.8 %all-to-all-start.1 = ((bf16[4,16,256,128]{3,2,1,0:T(8,128)(2,1)}), bf16[4,16,256,128]{3,2,1,0:T(8,128)(2,1)}, u32[]{:S(2)}, u32[]{:S(2)}) async-start(bf16[4,16,256,128]{3,2,1,0:T(8,128)(2,1)} %reshape.383), calls=%async_computation.4 | async-start | bytes 8388608 | tf_op jit(solution)/shard_map/all_to_all | solution.py:243
  341.3 122.9 %reduce-scatter.8.cloned.1.call-start = ((), (), s32[]{:S(2)}) async-start(), calls=%async_computation.8 | async-start | bytes 4718592 | tf_op jit(solution)/shard_map/reduce_scatter | solution.py:263
  343.6 6.1 %copy-start.13 = (f32[512]{0:T(512)S(1)}, f32[512]{0:T(512)}, u32[]{:S(2)}) copy-start(f32[512]{0:T(512)} %param.38) | copy-start | bytes 6148
  343.6 6.1 %copy-start.14 = (f32[512]{0:T(512)S(1)}, f32[512]{0:T(512)}, u32[]{:S(2)}) copy-start(f32[512]{0:T(512)} %param.37) | copy-start | bytes 6148
  402.1 0.7 copy-start.15
  402.1 0.7 copy-start.17
  453.2 13.1 %copy-start.1 = (bf16[4096,160]{0,1:T(8,128)(2,1)S(1)}, bf16[4096,160]{0,1:T(8,128)(2,1)}, u32[]{:S(2)}) copy-start(bf16[4096,160]{0,1:T(8,128)(2,1)} %param.26) | copy-start | bytes 3932164
  457.6 6.6 %copy-start.3 = (bf16[4,16,4096]{2,1,0:T(8,128)(2,1)S(1)}, bf16[4,16,4096]{2,1,0:T(8,128)(2,1)}, u32[]{:S(2)}) copy-start(bf16[4,16,4096]{2,1,0:T(8,128)(2,1)} %param.21) | copy-start | bytes 1572868
Sparse Core Ops, SparseCore 0:
  41.5 42.4 all-gather.6
  122.2 78.8 reduce-scatter.5
  203.6 77.2 reduce-scatter.3
  282.3 113.2 all-gather.4
  402.2 49.4 reduce-scatter.7
